TPU v7x, 256 devices: a whole 4x4x8 slice. The times are simulated.
256 devices in a mesh: seq: 32 (over x, y, core), grp: 8 (over z).
Axes of the slice: x: 4, y: 4, z: 8, core: 2. Of those that a mesh axis runs over, the one named last changes fastest.
Arguments:
- projected: bfloat16 [3, 8, 4096, 4096], P(None, 'grp', 'seq'), may hold values from -6 to 6
- short_filter: float32 [3, 3, 4096], replicated, may hold values from -3 to 3
- bias: float32 [4096], replicated, may hold values from -4 to 4
- residue: float32 [16, 4096], replicated, may hold values from -0.09375 to 0.09375
- rate: float32 [16, 4096], replicated, may hold values from 0.0001 to 0.05
- out_weight: bfloat16 [4096, 4096], P(None, 'grp'), may hold values from -0.09375 to 0.09375
Outputs:
- mixed: bfloat16 [8, 4096, 4096], P(None, 'seq', 'grp')
All inputs are finite; a program needn't handle non-finite values.
Results may differ from a plain program's by a relative error of at most 0.017.
Values may be sent and summed in bfloat16 or wider, within the bound.
A program may use at most 320 MiB of HBM per device.

v0:
```python
import math

import jax
import jax.numpy as jnp
from jax import lax
from jax.sharding import PartitionSpec as P

TWO_PI = 2.0 * math.pi


def passed_along(value, axis, steps):
    count = lax.axis_size(axis)
    initial, last = (max(0, -steps), min(count, count - steps))
    return lax.ppermute(value, axis, [(source, source + steps) for source in range(initial, last)])


def shortened(shard):
    return jax.tree.map(lambda a: a.astype(jnp.bfloat16) if a.dtype == jnp.float32 else a, shard)


def phases(numbers, period):
    turns = (numbers % period).astype(jnp.float32) * (TWO_PI / period)
    return (jnp.cos(turns), jnp.sin(turns))


def contract(table, values):
    return jnp.einsum("kb,bnd->knd", table, values, precision=lax.Precision.HIGHEST)


def along_rows(table, values):
    return jnp.einsum("qr,ard->aqd", table, values, precision=lax.Precision.HIGHEST)


def modal_spectrum(frequencies, residue, rate, transform_size, length):
    cosine, sine_val = phases(frequencies, transform_size)
    half_cos, half_sin = phases(frequencies, 2 * transform_size)
    parity_sign = (1 - 2 * (frequencies % 2)).astype(jnp.float32)[:, None]
    cosine = cosine[:, None]
    sine_val = sine_val[:, None]
    half_square = 2.0 * half_sin[:, None] * half_sin[:, None]
    real_spec = jnp.zeros((frequencies.shape[0], residue.shape[1]), jnp.float32)
    imag_spec = jnp.zeros((frequencies.shape[0], residue.shape[1]), jnp.float32)
    for mode_index in range(residue.shape[0]):
        weight_row = residue[mode_index][None, :]
        rate_row = rate[mode_index][None, :]
        numerator = 1.0 - parity_sign * jnp.exp(-rate_row * length)
        real_den = half_square + cosine * -jnp.expm1(-rate_row)
        imag_den = jnp.exp(-rate_row) * sine_val
        weighted = weight_row * numerator / (real_den * real_den + imag_den * imag_den)
        real_spec = real_spec + weighted * real_den
        imag_spec = imag_spec - weighted * imag_den
    return (real_spec, imag_spec)


def filtered_spectrum(real_freq, imag_freq, orders_here, residue, rate, transform_size, length):
    row_count = real_freq.shape[1]
    all_rows = jnp.arange(row_count, dtype=jnp.int32)
    cos_r, sin_r = phases(all_rows[:, None] * all_rows[None, :], row_count)
    real_z = along_rows(cos_r, real_freq) + along_rows(sin_r, imag_freq)
    imag_z = along_rows(cos_r, imag_freq) - along_rows(sin_r, real_freq)
    frequencies = (orders_here[:, None] + 2 * (length // row_count) * all_rows[None, :]).reshape(-1)
    real_h, imag_h = modal_spectrum(frequencies, residue, rate, transform_size, length)
    real_h = real_h.reshape(real_z.shape)
    imag_h = imag_h.reshape(real_z.shape)
    real_y = real_z * real_h - imag_z * imag_h
    imag_y = real_z * imag_h + imag_z * real_h
    real_b = along_rows(cos_r, real_y) - along_rows(sin_r, imag_y)
    imag_b = along_rows(cos_r, imag_y) + along_rows(sin_r, real_y)
    cos_i, sin_i = phases(orders_here[:, None, None] * all_rows[None, :, None], transform_size)
    real_c = real_b * cos_i - imag_b * sin_i
    imag_c = real_b * sin_i + imag_b * cos_i
    return (real_c, imag_c)


def on_device(projected, short_filter, bias, residue, rate, out_weight):
    part_count = lax.axis_size("seq")
    rank_here = lax.axis_index("seq")
    tap_count = short_filter.shape[1]
    row_count = projected.shape[2]
    piece_rows = row_count // part_count
    length = row_count * part_count
    transform_size = 2 * length
    edge_rows = projected[:, :, row_count - (tap_count - 1) :, :]
    before = passed_along(edge_rows, "seq", 1)
    extended = jnp.concatenate([before, projected], axis=2).astype(jnp.float32)
    featured = short_filter[:, 0][:, None, None, :] * extended[:, :, tap_count - 1 :, :]
    for offset in range(1, tap_count):
        featured = (
            featured
            + short_filter[:, offset][:, None, None, :]
            * extended[:, :, tap_count - 1 - offset : tap_count - 1 - offset + row_count, :]
        )
    queries = featured[0, 0]
    product = featured[1, 0] * featured[2, 0]
    local_rows = rank_here * piece_rows + jnp.arange(piece_rows, dtype=jnp.int32)
    blocks = jnp.arange(part_count, dtype=jnp.int32)
    orders = jnp.arange(2 * part_count, dtype=jnp.int32)
    columns = lax.all_to_all(
        product[None].astype(jnp.bfloat16), "seq", split_axis=1, concat_axis=0, tiled=True
    ).astype(jnp.float32)
    cos_b, sin_b = phases(orders[:, None] * blocks[None, :], 2 * part_count)
    real_x = contract(cos_b, columns)
    imag_x = -contract(sin_b, columns)
    cos_t, sin_t = phases(orders[:, None, None] * local_rows[None, :, None], transform_size)
    twisted = jnp.stack([real_x * cos_t + imag_x * sin_t, imag_x * cos_t - real_x * sin_t])
    spectra = lax.all_to_all(
        shortened(twisted), "seq", split_axis=1, concat_axis=2, tiled=True
    ).astype(twisted.dtype)
    orders_here = 2 * rank_here + jnp.arange(2, dtype=jnp.int32)
    real_c, imag_c = filtered_spectrum(
        spectra[0], spectra[1], orders_here, residue, rate, transform_size, length
    )
    regrouped = lax.all_to_all(
        shortened(jnp.stack([real_c, imag_c])), "seq", split_axis=2, concat_axis=1, tiled=True
    )
    cos_y, sin_y = phases(blocks[:, None] * orders[None, :], 2 * part_count)
    signal = (contract(cos_y, regrouped[0]) - contract(sin_y, regrouped[1])) / transform_size
    convolved = lax.all_to_all(
        shortened(signal), "seq", split_axis=0, concat_axis=1, tiled=True
    ).astype(signal.dtype)[0]
    gated = (queries * (convolved + bias[None, :] * product)).astype(jnp.bfloat16)
    return jnp.einsum(
        "srd,de->sre",
        lax.all_gather(gated[None], "grp", axis=0, tiled=True),
        out_weight,
        preferred_element_type=jnp.float32,
    ).astype(jnp.bfloat16)


def solution(mesh):
    placed = (P(None, "grp", "seq", None), P(), P(), P(), P(), P(None, "grp"))
    return jax.shard_map(
        on_device, mesh=mesh, in_specs=placed, out_specs=P(None, "seq", "grp"), check_vma=False
    )
```

profile of v0, /device:TPU:1, one launch (start us, length us, event | category | flops | bytes accessed | tf_op | source)
XLA Modules:
  0.0 464.0 jit_solution(13635082327341479827)
XLA Ops:
  6.5 1.0 slice.143
  7.5 4.6 collective-permute-start
  12.1 1.3 fusion.203
  13.5 0.1 copy_bitcast_fusion.1
  13.6 2.9 maximum_convert_fusion
  16.5 1.9 fusion
  18.4 0.2 fusion.69
  18.6 2.4 copy.53
  21.0 0.1 copy-done
  21.0 0.5 broadcast.1316
  21.5 7.0 %reduce.2 = bf16[128,4096]{1,0:T(8,128)(2,1)S(1)} reduce(bf16[128,1,4096]{2,1,0:T(2,128)(2,1)S(1)} %bitcast.176, bf16[]{:T(256)} %broadcast.1316), dimensions={1}, to_apply=%bitcast.173.reduce_sub_computation | reduce | bytes 2097154
  28.6 1.6 reshape.1647
  30.2 8.5 %all-to-all-start = ((bf16[32,2,8192]{2,1,0:T(2,128)(2,1)}), bf16[32,2,8192]{2,1,0:T(2,128)(2,1)S(1)}, u32[]{:S(2)}, u32[]{:S(2)}) async-start(bf16[32,2,8192]{2,1,0:T(2,128)(2,1)} %reshape.1647), calls=%async_computation | async-start | bytes 2097152 | tf_op jit(solution)/shard_map/all_to_all | solution.py:98
  38.7 0.3 fusion.75.clone.4
  39.0 0.1 fusion.130
  39.1 16.4 %all-to-all-done = bf16[32,2,8192]{2,1,0:T(2,128)(2,1)S(1)} async-done(((bf16[32,2,8192]{2,1,0:T(2,128)(2,1)}), bf16[32,2,8192]{2,1,0:T(2,128)(2,1)S(1)}, u32[]{:S(2)}, u32[]{:S(2)}) %all-to-all-start) | async-done | bytes 1048608 | tf_op jit(solution)/shard_map/all_to_all | solution.py:98
  55.5 1.0 reshape.1648
  56.5 6.2 %bitcast_reduce_fusion = bf16[128,4096]{1,0:T(8,128)(2,1)S(1)} fusion(bf16[128,1,4096]{2,1,0:T(2,128)(2,1)S(1)} %reshape.1648), kind=kLoop, calls=%fused_computation.340 | loop fusion | bytes 2097152 | tf_op jit(solution)/shard_map/all_to_all | solution.py:98
  62.8 0.6 all_to_all.19
  63.4 2.7 convolution_negate_fusion
  66.1 3.7 fusion.56
  69.8 0.4 pad_maximum_fusion
  70.2 5.3 %copy.25 = bf16[2,64,4,4096]{3,2,0,1:T(4,128)(2,1)} copy(bf16[2,64,4,4096]{3,1,2,0:T(8,128)(2,1)S(1)} %pad_maximum_fusion) | data formatting | bytes 8388608 | tf_op jit(solution)/shard_map/stack | solution.py:105
  75.4 4.8 %all-to-all-start.1 = ((bf16[2,64,4,4096]{3,2,0,1:T(4,128)(2,1)}), bf16[2,64,4,4096]{3,2,0,1:T(4,128)(2,1)}, u32[]{:S(2)}, u32[]{:S(2)}) async-start(bf16[2,64,4,4096]{3,2,0,1:T(4,128)(2,1)} %copy.25), calls=%async_computation.1 | async-start | bytes 8388608 | tf_op jit(solution)/shard_map/all_to_all | solution.py:106
  80.2 0.3 all-gather.2.cloned.1.call-start
  80.5 0.1 subtract_convert_fusion.2
  80.6 0.7 fusion.132
  81.3 0.2 multiply_exponential_fusion.14
  81.5 0.8 fusion.202
  82.4 1.1 multiply_exponential_fusion.15
  83.5 1.1 exponential-minus-one_negate_fusion.15
  84.6 47.8 %all-to-all-done.1 = bf16[2,64,4,4096]{3,2,0,1:T(4,128)(2,1)} async-done(((bf16[2,64,4,4096]{3,2,0,1:T(4,128)(2,1)}), bf16[2,64,4,4096]{3,2,0,1:T(4,128)(2,1)}, u32[]{:S(2)}, u32[]{:S(2)}) %all-to-all-start.1) | async-done | bytes 4194336 | tf_op jit(solution)/shard_map/all_to_all | solution.py:106
  132.5 6.6 %copy.51 = bf16[2,32,2,4,4096]{4,2,3,1,0:T(2,128)(2,1)S(1)} copy(bf16[2,32,2,4,4096]{4,3,0,2,1:T(4,128)(2,1)} %bitcast.7) | data formatting | bytes 8388608 | tf_op jit(solution)/shard_map/all_to_all | solution.py:106
  139.0 4.6 fusion.201
  143.6 4.1 copy.27
  147.7 4.9 %copy.28 = bf16[2,128,4096]{1,2,0:T(8,128)(2,1)S(1)} copy(bf16[2,128,4096]{2,0,1:T(2,128)(2,1)} %bitcast.177) | data formatting | bytes 4194304 | tf_op jit(solution)/shard_map/squeeze | solution.py:111
  152.6 2.0 fusion.81
  154.7 2.1 fusion.83
  157.1 0.0 copy-start.29
  157.2 2.2 fusion.3
  159.8 43.0 %multiply_subtract_fusion = (f32[2,128,4096]{1,2,0:T(8,128)S(1)}, f32[2,128,4096]{1,2,0:T(8,128)S(1)}, f32[2,128,4096]{1,2,0:T(8,128)}, f32[2,128,4096]{1,2,0:T(8,128)}) fusion(f32[2,128,4096]{1,2,0:T(8,128)S(1)} %fusion.3, f32[4096]{0:T(1024)S(1)} %bitcast.227, f32[4096]{0:T(1024)S(1)} %bitcast.226, f32[4096]{0:T(1024)S(1)} %bitcast.188, ...), kind=kOutput, calls=%fused_computation.103 | convolution fusion | flops 1848639488 | bytes 28381184 | tf_op jit(solution)/shard_map/qr,ard->aqd/dot_general | solution.py:31
  202.8 5.4 %multiply_add_fusion = f32[2,128,4096]{1,2,0:T(8,128)S(1)} fusion(f32[2,128,4096]{1,2,0:T(8,128)} %get-tuple-element.93, f32[2,128,4096]{1,2,0:T(8,128)} %get-tuple-element.7, f32[2,128,4096]{1,2,0:T(8,128)} %copy-done.2, f32[2,128,4096]{1,2,0:T(8,128)S(1)} %get-tuple-element.6), kind=kLoop, calls=%fused_computation.102 | loop fusion | flops 3145728 | bytes 20971520 | tf_op jit(solution)/shard_map/add | solution.py:66
  208.2 3.8 fusion.77
  212.0 3.9 fusion.79
  215.9 4.2 convolution_add_fusion
  220.2 5.1 %fusion.58 = (bf16[1,2,128,4096]{2,3,1,0:T(8,128)(2,1)S(1)}, bf16[1,2,128,4096]{2,3,1,0:T(8,128)(2,1)S(1)}) fusion(f32[2,4096,128]{2,1,0:T(8,128)S(1)} %convolution_add_fusion, f32[2,128]{1,0:T(2,128)S(1)} %copy-done.46, f32[2,128]{1,0:T(2,128)S(1)} %copy-done.45, f32[2,4096,128]{2,1,0:T(8,128)S(1)} %fusion.79, f32[2,128,4096]{1,2,0:T(8,128)S(1)} %multiply_add_fusion), kind=kOutput, calls=%fused_computation.126 | convolution fusion | flops 1620279296 | bytes 16779264 | tf_op jit(solution)/shard_map/qr,ard->aqd/dot_general | solution.py:31
  225.3 2.4 pad_maximum_fusion.1
  227.7 11.2 %copy.31 = bf16[2,2,128,4096]{3,1,0,2:T(2,128)(2,1)} copy(bf16[2,2,128,4096]{2,3,1,0:T(8,128)(2,1)} %pad_maximum_fusion.1) | data formatting | bytes 8388608 | tf_op jit(solution)/shard_map/stack | solution.py:114
  238.9 57.8 %all_to_all.51 = bf16[2,2,128,4096]{3,1,0,2:T(2,128)(2,1)} all-to-all(bf16[2,2,128,4096]{3,1,0,2:T(2,128)(2,1)} %copy.31), channel_id=1, replica_groups=mesh['seq'=32,'grp'=8] {'seq'}, dimensions={2} | all-to-all | bytes 8388608 | tf_op jit(solution)/shard_map/all_to_all | solution.py:113
  296.8 6.3 %copy.32 = bf16[2,2,128,4096]{3,1,2,0:T(2,128)(2,1)S(1)} copy(bf16[2,2,128,4096]{3,1,0,2:T(2,128)(2,1)} %all_to_all.51) | data formatting | bytes 8388608 | tf_op jit(solution)/shard_map/all_to_all | solution.py:113
  303.1 4.2 fusion.200
  307.3 3.3 copy.34
  310.6 2.7 squeeze.22
  313.3 5.5 %copy.33 = bf16[1,32,2,4,4096]{4,2,1,3,0:T(2,128)(2,1)} copy(bf16[1,32,2,4,4096]{4,2,3,1,0:T(2,128)(2,1)} %get-tuple-element.13) | data formatting | bytes 4194304 | tf_op jit(solution)/shard_map/slice | solution.py:117
  318.8 4.4 squeeze.21
  323.3 2.7 fusion.107
  325.9 1.2 fusion.5
  327.2 0.8 copy.35
  328.0 20.7 %all_to_all.52 = bf16[32,4,4096]{2,1,0:T(4,128)(2,1)S(1)} all-to-all(bf16[32,4,4096]{2,1,0:T(4,128)(2,1)S(1)} %copy.35), channel_id=1, replica_groups=mesh['seq'=32,'grp'=8] {'seq'}, dimensions={0} | all-to-all | bytes 2097152 | tf_op jit(solution)/shard_map/all_to_all | solution.py:118
  348.6 0.2 reshape.1638
  348.8 4.4 fusion.62
  353.2 0.0 all-gather.2.cloned.1.call-update
  353.3 93.5 %all-gather.2.cloned.1.call-done = bf16[8,128,4096]{2,1,0:T(8,128)(2,1)} async-done(((bf16[1,128,4096]{2,1,0:T(8,128)(2,1)}), bf16[8,128,4096]{2,1,0:T(8,128)(2,1)}) %all-gather.2.cloned.1.call-update) | async-done | bytes 8388624 | tf_op jit(solution)/shard_map/all_gather | solution.py:124
  446.7 10.0 %fusion.63 = bf16[8,128,512]{2,1,0:T(8,128)(2,1)} fusion(bf16[8,128,4096]{2,1,0:T(8,128)(2,1)} %all-gather.2.cloned.1.call-done, bf16[4096,512]{1,0:T(8,128)(2,1)} %param.11), kind=kOutput, calls=%fused_computation.133 | convolution fusion | flops 4295491584 | bytes 13631488 | tf_op jit(solution)/shard_map/srd,de->sre/dot_general | solution.py:122
  (97 shorter events, 0.2 us)
Async XLA Ops:
  7.5 6.1 %collective-permute-start = (bf16[3,1,2,4096]{3,2,1,0:T(2,128)(2,1)S(1)}, bf16[3,1,2,4096]{3,2,1,0:T(2,128)(2,1)S(1)}, u32[]{:S(2)}, u32[]{:S(2)}) collective-permute-start(bf16[3,1,2,4096]{3,2,1,0:T(2,128)(2,1)S(1)} %slice.143), channel_id=1, source_target_pairs={{0,8},{8,16},{16,24},{24,32},{32,40},{40,48},{48,56},{56,64},{64,7... | collective-permute-start | bytes 147464 | tf_op jit(solution)/shard_map/ppermute | solution.py:14
  18.4 2.7 copy-start
  30.2 25.3 %all-to-all-start = ((bf16[32,2,8192]{2,1,0:T(2,128)(2,1)}), bf16[32,2,8192]{2,1,0:T(2,128)(2,1)S(1)}, u32[]{:S(2)}, u32[]{:S(2)}) async-start(bf16[32,2,8192]{2,1,0:T(2,128)(2,1)} %reshape.1647), calls=%async_computation | async-start | bytes 2097152 | tf_op jit(solution)/shard_map/all_to_all | solution.py:98
  75.4 5.9 %copy-start.3 = (f32[16,4096]{1,0:T(8,128)S(1)}, f32[16,4096]{1,0:T(8,128)}, u32[]{:S(2)}) copy-start(f32[16,4096]{1,0:T(8,128)} %param.10) | copy-start | bytes 786436
  75.4 6.1 %copy-start.4 = (f32[16,4096]{1,0:T(8,128)S(1)}, f32[16,4096]{1,0:T(8,128)}, u32[]{:S(2)}) copy-start(f32[16,4096]{1,0:T(8,128)} %param.9) | copy-start | bytes 786436
  75.4 57.0 %all-to-all-start.1 = ((bf16[2,64,4,4096]{3,2,0,1:T(4,128)(2,1)}), bf16[2,64,4,4096]{3,2,0,1:T(4,128)(2,1)}, u32[]{:S(2)}, u32[]{:S(2)}) async-start(bf16[2,64,4,4096]{3,2,0,1:T(4,128)(2,1)} %copy.25), calls=%async_computation.1 | async-start | bytes 8388608 | tf_op jit(solution)/shard_map/all_to_all | solution.py:106
  80.2 366.5 %all-gather.2.cloned.1.call-start = ((), (), s32[]{:S(2)}) async-start(), calls=%async_computation.4 | async-start | bytes 9437184 | tf_op jit(solution)/shard_map/all_gather | solution.py:124
  152.6 2.1 copy-start.1
  156.8 2.6 copy-start.6
  156.8 2.6 copy-start.7
  156.8 2.6 copy-start.8
  156.9 2.6 copy-start.9
  156.9 2.6 copy-start.10
  156.9 2.6 copy-start.11
  156.9 2.6 copy-start.12
  156.9 2.6 copy-start.13
  156.9 2.6 copy-start.14
  156.9 2.6 copy-start.15
  156.9 2.6 copy-start.16
  156.9 2.6 copy-start.17
  156.9 2.6 copy-start.18
  157.0 2.6 copy-start.19
  157.0 2.6 copy-start.20
  157.0 2.6 copy-start.21
  157.0 2.6 copy-start.22
  157.0 2.6 copy-start.23
  157.0 2.6 copy-start.24
  157.0 2.6 copy-start.25
  157.0 2.6 copy-start.26
  157.0 2.6 copy-start.27
  157.0 2.6 copy-start.28
  157.1 2.6 copy-start.29
  157.1 2.6 copy-start.30
  157.1 2.6 copy-start.31
  157.1 2.6 copy-start.32
  157.1 2.6 copy-start.33
  157.1 2.6 copy-start.34
  157.1 2.6 copy-start.35
  157.1 2.6 copy-start.36
  157.1 2.6 copy-start.37
  157.1 2.6 copy-start.38
  157.2 2.6 copy-start.39
  157.2 2.6 copy-start.40
  157.2 2.6 copy-start.41
  157.2 2.6 copy-start.42
  157.2 2.6 copy-start.43
  157.2 2.6 copy-start.44
  159.4 43.4 %copy-start.2 = (f32[2,128,4096]{1,2,0:T(8,128)}, f32[2,128,4096]{1,2,0:T(8,128)S(1)}, u32[]{:S(2)}) copy-start(f32[2,128,4096]{1,2,0:T(8,128)S(1)} %fusion.3) | copy-start | bytes 12582916
  215.9 4.3 copy-start.45
  215.9 4.3 copy-start.46
  327.2 21.7 %copy-start.5 = (f32[4096]{0:T(1024)S(1)}, f32[4096]{0:T(1024)}, u32[]{:S(2)}) copy-start(f32[4096]{0:T(1024)} %param.8) | copy-start | bytes 49156
Sparse Core Ops, SparseCore 0:
  353.4 93.3 all-gather.1
where the time goes:
time: 473 us; the launch traced here: 464 us
  waiting for transfers between devices  158 us (33%)
  matrix products  86.6 us (18%)
  local copies, waits for them, and re-layouts  80 us (17%)
  blocking collectives  78.5 us (17%)
  other arithmetic  28.2 us (6%)
  starting transfers between devices  18.1 us (4%)
  between operations  14.9 us (3%)
    all_gather x1, waiting for transfers between devices, on_device(): lax.all_gather(gated[None], 'grp', axis=0, tiled=True)  93.5 us
    dot_general x8, matrix products, along_rows(): jnp.einsum('qr,ard->aqd', table, values, precision=lax.Precision.HIGHEST)  66.3 us
    all_to_all x1, blocking collectives, on_device(): lax.all_to_all(shortened(jnp.stack([real_c, imag_c])), 'seq', split_axis=...  57.8 us
    all_to_all x1, waiting for transfers between devices, on_device(): lax.all_to_all(shortened(twisted), 'seq', split_axis=1, concat_axis=2, ti...  47.8 us
    all_to_all x1, blocking collectives, on_device(): lax.all_to_all(shortened(signal), 'seq', split_axis=0, concat_axis=1, til...  20.7 us
    all_to_all x1, waiting for transfers between devices, on_device(): lax.all_to_all(product[None].astype(jnp.bfloat16), 'seq', split_axis=1, c...  16.4 us
    another operation x1, local copies, waits for them, and re-layouts, on_device(): jnp.stack([real_c, imag_c])  11.2 us
    dot_general x4, matrix products, contract(): jnp.einsum('kb,bnd->knd', table, values, precision=lax.Precision.HIGHEST)  10.2 us
  transfers between devices with their start and end apart: 4, of which 3 were waited for; matrix products, arithmetic and copies ran while one was open for 1% of the time, Pallas kernels for 0%

commit v1 on v0

v1 whole, which is shorter than its diff:
```python
import functools

import jax
import jax.numpy as jnp
from jax import lax
from jax.experimental import pallas as pl
from jax.experimental.pallas import tpu as pltpu
from jax.sharding import PartitionSpec as P

LANES = 128
GROUPS = 8
MIB = 1024 * 1024


def wide(row):
    return jnp.broadcast_to(row, (GROUPS, LANES))


def first_pass(lanes, steps, modes, halo, projected, taps, rate, extended, queries, product, starts, ends):
    count = steps * GROUPS
    for c in range(3):
        extended[c, pl.ds(0, 8), :] = halo[c, :, lanes].astype(jnp.float32)
        extended[c, pl.ds(8, count), :] = projected[c, :, lanes].astype(jnp.float32)
    decay = [wide(jnp.exp(-rate[pl.ds(m, 1), lanes])) for m in range(modes)]
    tap = [[wide(taps[c, pl.ds(j, 1), lanes]) for j in range(3)] for c in range(3)]
    state = [None] * modes
    held = [[extended[c, pl.ds(8 - j, GROUPS, stride=steps), :] for j in (2, 1)] for c in range(3)]
    for i in range(steps):
        featured = []
        for c in range(3):
            now = extended[c, pl.ds(8 + i, GROUPS, stride=steps), :]
            featured.append(tap[c][0] * now + tap[c][1] * held[c][1] + tap[c][2] * held[c][0])
            held[c] = [held[c][1], now]
        x = featured[1] * featured[2]
        queries[i, :, lanes] = featured[0]
        product[i, :, lanes] = x
        for m in range(modes):
            state[m] = x if i == 0 else decay[m] * state[m] + x
    row = lax.broadcasted_iota(jnp.int32, (GROUPS, LANES), 0)
    for m in range(modes):
        here = state[m]
        speed = wide(rate[pl.ds(m, 1), lanes])
        for distance in (1, 2, 4):
            factor = jnp.where(row >= distance, jnp.exp(speed * (-float(steps * distance))), 0.0)
            here = here + factor * pltpu.roll(here, distance, 0)
        starts[m, :, lanes] = jnp.where(row >= 1, pltpu.roll(here, 1, 0), 0.0)
        ends[pl.ds(m, 1), lanes] = here[GROUPS - 1 :, :]


def second_pass(lanes, steps, modes, queries, product, starts, before, rate, residue, bias, ordered, gated):
    row = lax.broadcasted_iota(jnp.int32, (GROUPS, LANES), 0).astype(jnp.float32)
    decay, weight, state = [], [], []
    for m in range(modes):
        speed = wide(rate[pl.ds(m, 1), lanes])
        decay.append(jnp.exp(-speed))
        weight.append(wide(residue[pl.ds(m, 1), lanes]))
        carried = jnp.exp(speed * row * (-float(steps))) * wide(before[pl.ds(m, 1), lanes])
        state.append(starts[m, :, lanes] + carried)
    skip = wide(bias[pl.ds(0, 1), lanes])
    for i in range(steps):
        x = product[i, :, lanes]
        total = skip * x
        for m in range(modes):
            state[m] = decay[m] * state[m] + x
            total = total + weight[m] * state[m]
        ordered[pl.ds(i, GROUPS, stride=steps), :] = queries[i, :, lanes] * total
    gated[:, lanes] = ordered[...].astype(jnp.bfloat16)


def first_kernel(steps, modes, halo, projected, taps, rate, queries, product, starts, ends, extended):
    @pl.loop(0, projected.shape[-1] // LANES)
    def _(slab):
        lanes = pl.ds(pl.multiple_of(slab * LANES, LANES), LANES)
        first_pass(lanes, steps, modes, halo, projected, taps, rate, extended, queries, product, starts, ends)


def scan_kernel(rate, ends, before):
    factor = jnp.exp(-float(SPAN) * rate[...])
    carried = jnp.zeros_like(factor)
    for r in range(ends.shape[0]):
        before[r] = carried
        carried = factor * carried + ends[r]


SPAN = 128


def second_kernel(steps, modes, queries, product, starts, before, rate, residue, bias, gated, ordered):
    @pl.loop(0, gated.shape[-1] // LANES)
    def _(slab):
        lanes = pl.ds(pl.multiple_of(slab * LANES, LANES), LANES)
        second_pass(lanes, steps, modes, queries, product, starts, before, rate, residue, bias, ordered, gated)


def on_device(projected, short_filter, bias, residue, rate, out_weight):
    ranks = lax.axis_size("seq")
    rank = lax.axis_index("seq")
    taken = projected[:, 0]
    rows, width = taken.shape[1:]
    modes = rate.shape[0]
    steps = rows // GROUPS
    edge = taken[:, rows - 8 :, :]
    halo = lax.ppermute(edge, "seq", [(i, i + 1) for i in range(ranks - 1)])
    f32 = jnp.float32
    params = pltpu.CompilerParams(vmem_limit_bytes=40 * MIB)
    vmem = pl.BlockSpec(memory_space=pltpu.VMEM)
    block = lambda *lead: pl.BlockSpec(lead + (512,), lambda k: (0,) * len(lead) + (k,))
    queries, product, starts, ends = pl.pallas_call(
        functools.partial(first_kernel, steps, modes),
        grid=(width // 512,),
        in_specs=[block(3, 8), block(3, rows), block(3, 3), block(modes)],
        out_specs=[block(steps, GROUPS), block(steps, GROUPS), block(modes, GROUPS), block(modes)],
        out_shape=[
            jax.ShapeDtypeStruct((steps, GROUPS, width), f32),
            jax.ShapeDtypeStruct((steps, GROUPS, width), f32),
            jax.ShapeDtypeStruct((modes, GROUPS, width), f32),
            jax.ShapeDtypeStruct((modes, width), f32),
        ],
        scratch_shapes=[pltpu.VMEM((3, rows + 8, LANES), f32)],
        compiler_params=params,
    )(halo, taken, short_filter, rate)
    part = width // ranks
    spread = lax.all_to_all(
        jnp.moveaxis(ends.reshape(modes, ranks, part), 1, 0), "seq", split_axis=0, concat_axis=0, tiled=True
    )
    own = lax.dynamic_slice_in_dim(rate, rank * part, part, axis=1)
    before = pl.pallas_call(
        scan_kernel,
        in_specs=[vmem, vmem],
        out_specs=vmem,
        out_shape=jax.ShapeDtypeStruct((ranks, modes, part), f32),
        compiler_params=params,
    )(own, spread)
    before = lax.all_to_all(before, "seq", split_axis=0, concat_axis=0, tiled=True)
    before = jnp.moveaxis(before, 0, 1).reshape(modes, width)
    gated = pl.pallas_call(
        functools.partial(second_kernel, steps, modes),
        grid=(width // 512,),
        in_specs=[
            block(steps, GROUPS),
            block(steps, GROUPS),
            block(modes, GROUPS),
            block(modes),
            block(modes),
            block(modes),
            block(1),
        ],
        out_specs=block(rows),
        out_shape=jax.ShapeDtypeStruct((rows, width), jnp.bfloat16),
        scratch_shapes=[pltpu.VMEM((rows, LANES), f32)],
        compiler_params=params,
    )(queries, product, starts, before, rate, residue, bias[None])
    return jnp.einsum(
        "srd,de->sre",
        lax.all_gather(gated[None], "grp", axis=0, tiled=True),
        out_weight,
        preferred_element_type=jnp.float32,
    ).astype(jnp.bfloat16)


def solution(mesh):
    placed = (P(None, "grp", "seq", None), P(), P(), P(), P(), P(None, "grp"))
    return jax.shard_map(
        on_device, mesh=mesh, in_specs=placed, out_specs=P(None, "seq", "grp"), check_vma=False
    )
```

time: 473 us -> 180 us (0.38)
  the two profiles are of different devices: /device:TPU:1 before, /device:TPU:4 now
where the time goes in v1:
time: 180 us; the launch traced here: 179 us
  waiting for transfers between devices  109 us (61%)
  Pallas kernels  14.9 us (8%)
  between operations  13.5 us (8%)
  blocking collectives  12.5 us (7%)
  local copies, waits for them, and re-layouts  11.3 us (6%)
  matrix products  10 us (6%)
  starting transfers between devices  7.45 us (4%)
    all_gather x1, waiting for transfers between devices, on_device(): lax.all_gather(gated[None], 'grp', axis=0, tiled=True)  95.3 us
    all_to_all x1, blocking collectives, on_device(): lax.all_to_all(before, 'seq', split_axis=0, concat_axis=0, tiled=True)  12.5 us
    dot_general x1, matrix products, on_device(): jnp.einsum('srd,de->sre', lax.all_gather(gated[None], 'grp', axis=0, tile...  10 us
    unnamed x20, local copies, waits for them, and re-layouts  9.6 us
    pallas_call x1, Pallas kernels, on_device(): pl.pallas_call(functools.partial(first_kernel, steps, modes), grid=(width...  7.6 us
    pallas_call x1, Pallas kernels, on_device(): pl.pallas_call(functools.partial(second_kernel, steps, modes), grid=(widt...  7.26 us
    ppermute x1, waiting for transfers between devices, on_device(): halo = lax.ppermute(edge, 'seq', [(i, i + 1) for i in range(ranks - 1)])  7.17 us
    all_to_all x1, waiting for transfers between devices, on_device(): lax.all_to_all(jnp.moveaxis(ends.reshape(modes, ranks, part), 1, 0), 'seq...  6.92 us
  transfers between devices with their start and end apart: 3, of which 3 were waited for; matrix products, arithmetic and copies ran while one was open for 0% of the time, Pallas kernels for 0%

profile of v1, /device:TPU:4, one launch (start us, length us, event | category | flops | bytes accessed | tf_op | source)
XLA Modules:
  0.0 179.1 jit_solution(17032824504810015896)
XLA Ops:
  6.5 0.0 copy-start.6
  6.5 0.0 copy-start.9
  6.5 1.0 slice.4
  7.5 1.9 %collective-permute-start = (bf16[3,8,4096]{2,1,0:T(8,128)(2,1)S(1)}, bf16[3,8,4096]{2,1,0:T(8,128)(2,1)S(1)}, u32[]{:S(2)}, u32[]{:S(2)}) collective-permute-start(bf16[3,8,4096]{2,1,0:T(8,128)(2,1)S(1)} %slice.4), channel_id=1, source_target_pairs={{0,8},{8,16},{16,24},{24,32},{32,40},{40,48},{48,56},{56,64},{64,7... | collective-permute-start | bytes 589832 | tf_op jit(solution)/shard_map/ppermute | solution.py:103
  9.5 7.2 %collective-permute-done.halo = bf16[3,8,4096]{2,1,0:T(8,128)(2,1)S(1)} collective-permute-done((bf16[3,8,4096]{2,1,0:T(8,128)(2,1)S(1)}, bf16[3,8,4096]{2,1,0:T(8,128)(2,1)S(1)}, u32[]{:S(2)}, u32[]{:S(2)}) %collective-permute-start) | collective-permute-done | bytes 196640 | tf_op jit(solution)/shard_map/ppermute | solution.py:103
  16.6 0.0 copy-start
  16.6 1.9 %copy-done = bf16[3,1,128,4096]{3,2,1,0:T(8,128)(2,1)S(1)} copy-done((bf16[3,1,128,4096]{3,2,1,0:T(8,128)(2,1)S(1)}, bf16[3,1,128,4096]{3,2,1,0:T(8,128)(2,1)}, u32[]{:S(2)}) %copy-start) | copy-done | bytes 3145752
  18.5 0.0 copy-start.5
  18.5 0.9 copy-done.5
  19.5 0.0 copy-start.8
  19.5 0.9 copy-done.8
  20.4 0.0 copy-start.7
  20.4 7.6 %shard_map.64 = (f32[16,8,4096]{2,1,0:T(8,128)S(1)}, f32[16,8,4096]{2,1,0:T(8,128)S(1)}, f32[16,8,4096]{2,1,0:T(8,128)S(1)}, f32[16,4096]{1,0:T(8,128)S(1)}) custom-call(bf16[3,8,4096]{2,1,0:T(8,128)(2,1)S(1)} %collective-permute-done.halo, bf16[3,128,4096]{2,1,0:T(8,128)(2,1)S(1)} %bitcast.23, f32[3,3,4096]{2,1,0:T(4,128)S(1)} %copy-done.8, ...), custom_call_target="tpu_custom_call" | custom-call | tf_op jit(solution)/shard_map/pallas_call | solution.py:108
  28.0 0.0 copy-start.1
  28.0 1.3 copy-done.1
  29.3 0.0 copy-start.3
  29.3 1.3 copy-done.3
  30.7 0.7 bitcast_bitcast_fusion
  31.4 5.5 %all-to-all-start = ((f32[32,16,128]{2,1,0:T(8,128)}), f32[32,16,128]{2,1,0:T(8,128)S(1)}, u32[]{:S(2)}, u32[]{:S(2)}) async-start(f32[32,16,128]{2,1,0:T(8,128)} %bitcast_bitcast_fusion), calls=%async_computation | async-start | bytes 524288 | tf_op jit(solution)/shard_map/all_to_all | solution.py:123
  36.9 0.0 all-gather.3.cloned.1.call-start
  36.9 0.0 copy-done.6
  37.0 6.9 %all-to-all-done.ends = f32[32,16,128]{2,1,0:T(8,128)S(1)} async-done(((f32[32,16,128]{2,1,0:T(8,128)}), f32[32,16,128]{2,1,0:T(8,128)S(1)}, u32[]{:S(2)}, u32[]{:S(2)}) %all-to-all-start) | async-done | bytes 262176 | tf_op jit(solution)/shard_map/all_to_all | solution.py:123
  43.9 0.1 shard_map.65
  44.0 12.5 %all_to_all.10 = f32[32,16,128]{2,1,0:T(8,128)S(1)} all-to-all(f32[32,16,128]{2,1,0:T(8,128)S(1)} %shard_map.65), channel_id=1, replica_groups=mesh['seq'=32,'grp'=8] {'seq'}, dimensions={0} | all-to-all | bytes 524288 | tf_op jit(solution)/shard_map/all_to_all | solution.py:134
  56.4 0.0 copy-done.9
  56.4 0.0 copy-done.7
  56.5 0.0 copy-start.2
  56.5 1.6 copy-done.2
  58.0 0.0 copy-start.4
  58.1 1.6 copy-done.4
  59.6 7.3 %shard_map.66 = bf16[128,4096]{1,0:T(8,128)(2,1)} custom-call(f32[16,8,4096]{2,1,0:T(8,128)S(1)} %get-tuple-element.9.queries, f32[16,8,4096]{2,1,0:T(8,128)S(1)} %copy-done.2, f32[16,8,4096]{2,1,0:T(8,128)S(1)} %copy-done.4, f32[16,4096]{1,0:T(8,128)S(1)} %copy_bitcast_fusion.before, f32[16,4096]{1,0:T(8,128)S(1)} %copy-done.6, f32[16,4096]{1,0:T(8,128)S(1)} %copy-done.7, ...), custom_call_target="tpu_custom_call" | custom-call | tf_op jit(solution)/shard_map/pallas_call | solution.py:136
  66.9 0.0 all-gather.3.cloned.1.call-update
  66.9 95.3 %all-gather.3.cloned.1.call-done = bf16[1024,4096]{1,0:T(8,128)(2,1)} async-done(((bf16[128,4096]{1,0:T(8,128)(2,1)}), bf16[1024,4096]{1,0:T(8,128)(2,1)}) %all-gather.3.cloned.1.call-update) | async-done | bytes 8388624 | tf_op jit(solution)/shard_map/all_gather | solution.py:155
  162.2 10.0 %fusion.2 = bf16[8,128,512]{2,1,0:T(8,128)(2,1)} fusion(bf16[8,128,4096]{2,1,0:T(8,128)(2,1)} %bitcast.25, bf16[4096,512]{1,0:T(8,128)(2,1)} %param.11), kind=kOutput, calls=%fused_computation.2 | convolution fusion | flops 4295491584 | bytes 13631488 | tf_op jit(solution)/shard_map/srd,de->sre/dot_general | solution.py:153
  (2 shorter events, 0.0 us)
Async XLA Ops:
  6.5 30.4 %copy-start.6 = (f32[16,4096]{1,0:T(8,128)S(1)}, f32[16,4096]{1,0:T(8,128)}, u32[]{:S(2)}) copy-start(f32[16,4096]{1,0:T(8,128)} %rate.3) | copy-start | bytes 786436
  6.5 49.9 %copy-start.9 = (f32[4096]{0:T(1024)S(1)}, f32[4096]{0:T(1024)}, u32[]{:S(2)}) copy-start(f32[4096]{0:T(1024)} %param.8) | copy-start | bytes 49156
  7.5 9.1 %collective-permute-start = (bf16[3,8,4096]{2,1,0:T(8,128)(2,1)S(1)}, bf16[3,8,4096]{2,1,0:T(8,128)(2,1)S(1)}, u32[]{:S(2)}, u32[]{:S(2)}) collective-permute-start(bf16[3,8,4096]{2,1,0:T(8,128)(2,1)S(1)} %slice.4), channel_id=1, source_target_pairs={{0,8},{8,16},{16,24},{24,32},{32,40},{40,48},{48,56},{56,64},{64,7... | collective-permute-start | bytes 589832 | tf_op jit(solution)/shard_map/ppermute | solution.py:103
  16.6 1.9 %copy-start = (bf16[3,1,128,4096]{3,2,1,0:T(8,128)(2,1)S(1)}, bf16[3,1,128,4096]{3,2,1,0:T(8,128)(2,1)}, u32[]{:S(2)}) copy-start(bf16[3,1,128,4096]{3,2,1,0:T(8,128)(2,1)} %param.6) | copy-start | bytes 9437188
  18.5 0.9 copy-start.5
  19.5 0.9 copy-start.8
  20.4 36.1 %copy-start.7 = (f32[16,4096]{1,0:T(8,128)S(1)}, f32[16,4096]{1,0:T(8,128)}, u32[]{:S(2)}) copy-start(f32[16,4096]{1,0:T(8,128)} %residue.1) | copy-start | bytes 786436
  28.0 1.3 copy-start.1
  29.3 1.3 copy-start.3
  31.4 12.5 %all-to-all-start = ((f32[32,16,128]{2,1,0:T(8,128)}), f32[32,16,128]{2,1,0:T(8,128)S(1)}, u32[]{:S(2)}, u32[]{:S(2)}) async-start(f32[32,16,128]{2,1,0:T(8,128)} %bitcast_bitcast_fusion), calls=%async_computation | async-start | bytes 524288 | tf_op jit(solution)/shard_map/all_to_all | solution.py:123
  36.9 125.3 %all-gather.3.cloned.1.call-start = ((), (), s32[]{:S(2)}) async-start(), calls=%async_computation.2 | async-start | bytes 9437184 | tf_op jit(solution)/shard_map/all_gather | solution.py:155
  56.5 1.6 copy-start.2
  58.0 1.6 copy-start.4
Sparse Core Ops, SparseCore 0:
  67.0 95.1 all-gather.2

commit v2 on v1

v2 whole, which is shorter than its diff:
```python
import functools

import jax
import jax.numpy as jnp
from jax import lax
from jax.experimental import pallas as pl
from jax.experimental.pallas import tpu as pltpu
from jax.sharding import PartitionSpec as P

LANES = 128
GROUPS = 8
MIB = 1024 * 1024


MESH = pl.DeviceIdType.MESH


def slab_lanes(slab):
    return pl.ds(pl.multiple_of(slab * LANES, LANES), LANES)


def wide(row):
    return jnp.broadcast_to(row, (GROUPS, LANES))


def first_pass(slab, keep, steps, modes, halo, projected, taps, rate, extended, queries, product, starts, ends):
    lanes = slab_lanes(slab)
    count = steps * GROUPS
    for c in range(3):
        extended[c, pl.ds(6, 2), :] = halo[pl.ds(2 * c, 2), lanes] * keep
        extended[c, pl.ds(8, count), :] = projected[c, :, lanes].astype(jnp.float32)
    decay = [wide(jnp.exp(-rate[pl.ds(m, 1), lanes])) for m in range(modes)]
    tap = [[wide(taps[c, pl.ds(j, 1), lanes]) for j in range(3)] for c in range(3)]
    state = [None] * modes
    held = [[extended[c, pl.ds(8 - j, GROUPS, stride=steps), :] for j in (2, 1)] for c in range(3)]
    for i in range(steps):
        featured = []
        for c in range(3):
            now = extended[c, pl.ds(8 + i, GROUPS, stride=steps), :]
            featured.append(tap[c][0] * now + tap[c][1] * held[c][1] + tap[c][2] * held[c][0])
            held[c] = [held[c][1], now]
        x = featured[1] * featured[2]
        queries[i, :, lanes] = featured[0]
        product[i, :, lanes] = x
        for m in range(modes):
            state[m] = x if i == 0 else decay[m] * state[m] + x
    row = lax.broadcasted_iota(jnp.int32, (GROUPS, LANES), 0)
    for m in range(modes):
        here = state[m]
        speed = wide(rate[pl.ds(m, 1), lanes])
        for distance in (1, 2, 4):
            factor = jnp.where(row >= distance, jnp.exp(speed * (-float(steps * distance))), 0.0)
            here = here + factor * pltpu.roll(here, distance, 0)
        starts[m, :, lanes] = jnp.where(row >= 1, pltpu.roll(here, 1, 0), 0.0)
        ends[slab, pl.ds(m, 1), :] = here[GROUPS - 1 :, :]


def second_pass(slab, steps, modes, queries, product, starts, before, rate, residue, bias, ordered):
    lanes = slab_lanes(slab)
    row = lax.broadcasted_iota(jnp.int32, (GROUPS, LANES), 0).astype(jnp.float32)
    decay, weight, state = [], [], []
    for m in range(modes):
        speed = wide(rate[pl.ds(m, 1), lanes])
        decay.append(jnp.exp(-speed))
        weight.append(wide(residue[pl.ds(m, 1), lanes]))
        carried = jnp.exp(speed * row * (-float(steps))) * wide(before[slab, pl.ds(m, 1), :])
        state.append(starts[m, :, lanes] + carried)
    skip = wide(bias[pl.ds(0, 1), lanes])
    for i in range(steps):
        x = product[i, :, lanes]
        total = skip * x
        for m in range(modes):
            state[m] = decay[m] * state[m] + x
            total = total + weight[m] * state[m]
        ordered[pl.ds(i, GROUPS, stride=steps), :] = queries[i, :, lanes] * total
    return ordered[...].astype(jnp.bfloat16)


def front_kernel(
    ranks,
    steps,
    modes,
    projected,
    taps,
    rate,
    residue,
    bias,
    gated,
    extended,
    ordered,
    queries,
    product,
    starts,
    edge,
    halo,
    ends,
    spread,
    back,
    before,
    edge_sem,
    ends_sem,
    back_sem,
):
    rank = lax.axis_index("seq")
    column = lax.axis_index("grp")
    rows = steps * GROUPS

    barrier = pltpu.get_barrier_semaphore()

    @pl.loop(1, ranks)
    def _(i):
        pl.semaphore_signal(
            barrier, inc=1, device_id=(lax.rem(rank + i, ranks), column), device_id_type=MESH
        )

    for c in range(3):
        edge[pl.ds(2 * c, 2), :] = projected[c, pl.ds(rows - 16, 16), :].astype(jnp.float32)[14:, :]
    pl.semaphore_wait(barrier, ranks - 1)

    edge_copy = pltpu.make_async_remote_copy(
        src_ref=edge,
        dst_ref=halo,
        send_sem=edge_sem.at[0],
        recv_sem=edge_sem.at[1],
        device_id=(lax.rem(rank + 1, ranks), column),
        device_id_type=MESH,
    )
    edge_copy.start()
    edge_copy.wait_recv()
    keep = jnp.where(rank > 0, 1.0, 0.0)

    def ends_copy(owner):
        return pltpu.make_async_remote_copy(
            src_ref=ends.at[owner],
            dst_ref=spread.at[rank],
            send_sem=ends_sem.at[0],
            recv_sem=ends_sem.at[1],
            device_id=(owner, column),
            device_id_type=MESH,
        )

    @pl.loop(0, ranks)
    def _(slab):
        first_pass(slab, keep, steps, modes, halo, projected, taps, rate, extended, queries, product, starts, ends)

        @pl.when(slab == rank)
        def _():
            spread[rank] = ends[rank]

        @pl.when(slab != rank)
        def _():
            ends_copy(slab).start()

    def all_but_one(ref, send_sem, recv_sem):
        return pltpu.make_async_remote_copy(
            src_ref=ref.at[pl.ds(0, ranks - 1)],
            dst_ref=ref.at[pl.ds(0, ranks - 1)],
            send_sem=send_sem,
            recv_sem=recv_sem,
            device_id=(lax.rem(rank + 1, ranks), column),
            device_id_type=MESH,
        )

    all_but_one(spread, ends_sem.at[0], ends_sem.at[1]).wait_recv()
    factor = jnp.exp(rate[:, slab_lanes(rank)] * (-float(rows)))
    carried = jnp.zeros_like(factor)
    for r in range(ranks):
        back[r] = carried
        carried = factor * carried + spread[r]
    before[rank] = back[rank]

    @pl.loop(1, ranks)
    def _(i):
        other = lax.rem(rank + i, ranks)
        pltpu.make_async_remote_copy(
            src_ref=back.at[other],
            dst_ref=before.at[rank],
            send_sem=back_sem.at[0],
            recv_sem=back_sem.at[1],
            device_id=(other, column),
            device_id_type=MESH,
        ).start()

    all_but_one(before, back_sem.at[0], back_sem.at[1]).wait_recv()

    @pl.loop(0, ranks)
    def _(slab):
        gated[:, slab_lanes(slab)] = second_pass(
            slab, steps, modes, queries, product, starts, before, rate, residue, bias, ordered
        )

    edge_copy.wait_send()
    all_but_one(ends, ends_sem.at[0], ends_sem.at[1]).wait_send()
    all_but_one(back, back_sem.at[0], back_sem.at[1]).wait_send()


def on_device(projected, short_filter, bias, residue, rate, out_weight):
    ranks = lax.axis_size("seq")
    taken = projected[:, 0]
    rows, width = taken.shape[1:]
    modes = rate.shape[0]
    steps = rows // GROUPS
    f32 = jnp.float32
    vmem = pl.BlockSpec(memory_space=pltpu.VMEM)
    exchanged = pltpu.VMEM((ranks, modes, width // ranks), f32)
    gated = pl.pallas_call(
        functools.partial(front_kernel, ranks, steps, modes),
        in_specs=[vmem] * 5,
        out_specs=vmem,
        out_shape=jax.ShapeDtypeStruct((rows, width), jnp.bfloat16),
        scratch_shapes=[
            pltpu.VMEM((3, rows + 8, LANES), f32),
            pltpu.VMEM((rows, LANES), f32),
            pltpu.VMEM((steps, GROUPS, width), f32),
            pltpu.VMEM((steps, GROUPS, width), f32),
            pltpu.VMEM((modes, GROUPS, width), f32),
            pltpu.VMEM((8, width), f32),
            pltpu.VMEM((8, width), f32),
            exchanged,
            exchanged,
            exchanged,
            exchanged,
            pltpu.SemaphoreType.DMA((2,)),
            pltpu.SemaphoreType.DMA((2,)),
            pltpu.SemaphoreType.DMA((2,)),
        ],
        compiler_params=pltpu.CompilerParams(
            collective_id=0, has_side_effects=True, vmem_limit_bytes=48 * MIB
        ),
    )(taken, short_filter, rate, residue, bias[None])
    return jnp.einsum(
        "srd,de->sre",
        lax.all_gather(gated[None], "grp", axis=0, tiled=True),
        out_weight,
        preferred_element_type=jnp.float32,
    ).astype(jnp.bfloat16)


def solution(mesh):
    placed = (P(None, "grp", "seq", None), P(), P(), P(), P(), P(None, "grp"))
    return jax.shard_map(
        on_device, mesh=mesh, in_specs=placed, out_specs=P(None, "seq", "grp"), check_vma=False
    )
```

time: 180 us -> 160 us (0.89)
  Pallas kernels: 14.9 us -> 33.8 us
  waiting for transfers between devices: 109 us -> 96.2 us
  blocking collectives: 12.5 us -> 0 us
  starting transfers between devices: 7.45 us -> 0.01 us
  local copies, waits for them, and re-layouts: 11.3 us -> 5.43 us
    pallas_call x3 -> x1, Pallas kernels: 14.9 us -> 33.8 us  [on_device(): pl.pallas_call(functools.partial(front_kernel, ranks, steps, modes), in_s...]
    all_to_all x1 -> x0, blocking collectives: 12.5 us -> none  [on_device(): lax.all_to_all(before, 'seq', split_axis=0, concat_axis=0, tiled=True)]
    ppermute x1 -> x0, waiting for transfers between devices: 7.17 us -> none  [on_device(): halo = lax.ppermute(edge, 'seq', [(i, i + 1) for i in range(ranks - 1)])]
    all_to_all x1 -> x0, waiting for transfers between devices: 6.92 us -> none  [on_device(): lax.all_to_all(jnp.moveaxis(ends.reshape(modes, ranks, part), 1, 0), 'seq...]
    all_to_all x1 -> x0, starting transfers between devices: 5.49 us -> none  [on_device(): lax.all_to_all(jnp.moveaxis(ends.reshape(modes, ranks, part), 1, 0), 'seq...]
    unnamed x20 -> x10, local copies, waits for them, and re-layouts: 9.6 us -> 5.43 us
    ppermute x1 -> x0, starting transfers between devices: 1.92 us -> none  [on_device(): halo = lax.ppermute(edge, 'seq', [(i, i + 1) for i in range(ranks - 1)])]
  transfers between devices with their start and end apart: 3 -> 1, of which waited for: 3 -> 1; matrix products, arithmetic and copies ran while one was open for 0% -> 0% of each run, Pallas kernels for 0% -> 0%
where the time goes in v2:
time: 160 us; the launch traced here: 159 us
  waiting for transfers between devices  96.2 us (60%)
  Pallas kernels  33.8 us (21%)
  between operations  13.4 us (8%)
  matrix products  10 us (6%)
  local copies, waits for them, and re-layouts  5.43 us (3%)
    all_gather x1, waiting for transfers between devices, on_device(): lax.all_gather(gated[None], 'grp', axis=0, tiled=True)  96.1 us
    pallas_call x1, Pallas kernels, on_device(): pl.pallas_call(functools.partial(front_kernel, ranks, steps, modes), in_s...  33.8 us
    dot_general x1, matrix products, on_device(): jnp.einsum('srd,de->sre', lax.all_gather(gated[None], 'grp', axis=0, tile...  10 us
    unnamed x10, local copies, waits for them, and re-layouts  5.43 us
  transfers between devices with their start and end apart: 1, of which 1 were waited for; matrix products, arithmetic and copies ran while one was open for 0% of the time, Pallas kernels for 0%

profile of v2, /device:TPU:4, one launch (start us, length us, event | category | flops | bytes accessed | tf_op | source)
XLA Modules:
  0.0 158.8 jit_solution(9876870822707523040)
XLA Ops:
  6.5 0.0 all-gather.3.cloned.1.call-start
  6.5 0.0 copy-start
  6.5 1.9 %copy-done = bf16[3,1,128,4096]{3,2,1,0:T(8,128)(2,1)S(1)} copy-done((bf16[3,1,128,4096]{3,2,1,0:T(8,128)(2,1)S(1)}, bf16[3,1,128,4096]{3,2,1,0:T(8,128)(2,1)}, u32[]{:S(2)}) %copy-start) | copy-done | bytes 3145752
  8.4 0.0 copy-start.1
  8.4 0.9 copy-done.1
  9.4 0.0 copy-start.2
  9.4 0.9 copy-done.2
  10.3 0.0 copy-start.3
  10.3 0.9 copy-done.3
  11.3 0.0 copy-start.4
  11.3 0.7 copy-done.4
  12.0 33.8 %shard_map.64 = bf16[128,4096]{1,0:T(8,128)(2,1)} custom-call(bf16[3,128,4096]{2,1,0:T(8,128)(2,1)S(1)} %bitcast.9, f32[3,3,4096]{2,1,0:T(4,128)S(1)} %copy-done.3, f32[16,4096]{1,0:T(8,128)S(1)} %copy-done.1, f32[16,4096]{1,0:T(8,128)S(1)} %copy-done.2, f32[1,4096]{1,0:T(1,128)S(1)} %bitcast.10), custom_call_target="tpu_custom_call" | custom-call | tf_op jit(solution)/shard_map/pallas_call | solution.py:206
  45.8 0.0 all-gather.3.cloned.1.call-update
  45.8 96.1 %all-gather.3.cloned.1.call-done = bf16[1024,4096]{1,0:T(8,128)(2,1)} async-done(((bf16[128,4096]{1,0:T(8,128)(2,1)}), bf16[1024,4096]{1,0:T(8,128)(2,1)}) %all-gather.3.cloned.1.call-update) | async-done | bytes 8388624 | tf_op jit(solution)/shard_map/all_gather | solution.py:233
  141.9 10.0 %fusion.2 = bf16[8,128,512]{2,1,0:T(8,128)(2,1)} fusion(bf16[8,128,4096]{2,1,0:T(8,128)(2,1)} %bitcast.11, bf16[4096,512]{1,0:T(8,128)(2,1)} %param.11), kind=kOutput, calls=%fused_computation.2 | convolution fusion | flops 4295491584 | bytes 13631488 | tf_op jit(solution)/shard_map/srd,de->sre/dot_general | solution.py:231
Async XLA Ops:
  6.5 135.4 %all-gather.3.cloned.1.call-start = ((), (), s32[]{:S(2)}) async-start(), calls=%async_computation | async-start | bytes 9437184 | tf_op jit(solution)/shard_map/all_gather | solution.py:233
  6.5 1.9 %copy-start = (bf16[3,1,128,4096]{3,2,1,0:T(8,128)(2,1)S(1)}, bf16[3,1,128,4096]{3,2,1,0:T(8,128)(2,1)}, u32[]{:S(2)}) copy-start(bf16[3,1,128,4096]{3,2,1,0:T(8,128)(2,1)} %param.6) | copy-start | bytes 9437188
  8.4 0.9 copy-start.1
  9.4 0.9 copy-start.2
  10.3 0.9 copy-start.3
  11.3 0.7 copy-start.4
Sparse Core Ops, SparseCore 0:
  45.9 95.9 all-gather.2

commit v3 on v2

--- a/solution.py
+++ b/solution.py
@@ -76,7 +76,15 @@
     return ordered[...].astype(jnp.bfloat16)
 
 
-def front_kernel(
+BLOCKS = 4
+PARTS = 4
+CHUNKS = 8
+SHARED = 96
+SKEW = 2
+SCOPE = 4
+
+
+def block_kernel(
     ranks,
     steps,
     modes,
@@ -85,7 +93,8 @@
     rate,
     residue,
     bias,
-    gated,
+    out_weight,
+    mixed,
     extended,
     ordered,
     queries,
@@ -97,71 +106,178 @@
     spread,
     back,
     before,
+    weight,
+    gathered,
+    total,
+    leaving,
+    returned,
     edge_sem,
     ends_sem,
     back_sem,
+    left_sem,
+    right_sem,
+    swap_sem,
+    twin_sem,
+    sent_sem,
+    rows_sem,
+    return_sem,
+    mixed_sem,
 ):
     rank = lax.axis_index("seq")
-    column = lax.axis_index("grp")
+    z = lax.axis_index("grp")
+    depth = mixed.shape[0]
     rows = steps * GROUPS
+    x, y, core = rank // 8, (rank // 2) % 4, rank % 2
+    side = y % 2
+    q = (x + 2 * (y // 2)) % BLOCKS
+
+    def at(px, py, pcore):
+        return (px % 4) * 8 + (py % 4) * 2 + pcore
+
+    x_up, x_down = at(x + 1, y, core), at(x + 3, y, core)
+    y_out = at(x, y + 3 + 2 * side, core)
+    y_pair = at(x, y + 1 - 2 * side, core)
+    twin = at(x, y, 1 - core)
+
+    def remote(source, target, send_sem, recv_sem, to_rank, to_z):
+        return pltpu.make_async_remote_copy(
+            src_ref=source,
+            dst_ref=target,
+            send_sem=send_sem,
+            recv_sem=recv_sem,
+            device_id=(to_rank, to_z),
+            device_id_type=MESH,
+        )
 
     barrier = pltpu.get_barrier_semaphore()
 
     @pl.loop(1, ranks)
     def _(i):
-        pl.semaphore_signal(
-            barrier, inc=1, device_id=(lax.rem(rank + i, ranks), column), device_id_type=MESH
-        )
+        pl.semaphore_signal(barrier, inc=1, device_id=(lax.rem(rank + i, ranks), z), device_id_type=MESH)
+
+    @pl.loop(1, depth)
+    def _(i):
+        pl.semaphore_signal(barrier, inc=1, device_id=(rank, lax.rem(z + i, depth)), device_id_type=MESH)
+
+    up = (z + depth - q) % BLOCKS
+    down = (q + depth - z) % BLOCKS
+    from_above = ((z + down + depth - q) % depth) // BLOCKS
+    from_below = 1 - from_above
+    span = weight.shape[1] // CHUNKS
+    half = span // 2
+    taken = half - SHARED
+    count = PARTS * CHUNKS
+
+    def weight_rows(j, offset, size, block=None):
+        start = pl.multiple_of((j % CHUNKS) * span + core * half + offset, 16)
+        columns = pl.ds(0, 2 * LANES) if block is None else slab_lanes(block)
+        return weight.at[j // CHUNKS, pl.ds(start, size), columns]
+
+    def moving(j, block, send_sem, recv_sem, to_z):
+        view = weight_rows(j, side * SHARED, taken, block)
+        return remote(view, view, send_sem, recv_sem.at[j], rank, to_z % depth)
+
+    def upward(j, block):
+        return moving(j, block, sent_sem.at[0], left_sem, z + 1)
+
+    def downward(j, block):
+        return moving(j, block, sent_sem.at[1], right_sem, z + depth - 1)
+
+    def swap(j, block):
+        view = weight_rows(j, side * taken, SHARED, block)
+        return remote(view, view, sent_sem.at[2], swap_sem.at[j], y_pair, z)
+
+    def weight_step(n):
+        j = n - SKEW * down
+
+        @pl.when((j >= 0) & (j < count))
+        def _():
+            downward(j, from_above).wait_recv()
+
+            @pl.when(down < BLOCKS - 1)
+            def _():
+                downward(j, from_above).start()
+
+            @pl.when(up == 0)
+            def _():
+                upward(j, from_above).start()
+
+            swap(j, from_above).start()
+
+        k = n - SKEW * jnp.where(up == 0, BLOCKS, up)
+
+        @pl.when((k >= 0) & (k < count))
+        def _():
+            upward(k, from_below).wait_recv()
+
+            @pl.when(up > 0)
+            def _():
+                upward(k, from_below).start()
+
+            swap(k, from_below).start()
+
+        whole = n - SKEW * (BLOCKS + 1)
+
+        @pl.when((whole >= 0) & (whole < count))
+        def _():
+            other = weight_rows(whole, (1 - side) * taken, SHARED)
+            remote(other, other, sent_sem.at[2], swap_sem.at[whole], y_pair, z).wait_recv()
+            view = weight_rows(whole, 0, half)
+            remote(view, view, sent_sem.at[3], twin_sem.at[whole // CHUNKS], twin, z).start()
+
+    def weight_steps(first, last):
+        @pl.loop(first, last)
+        def _(n):
+            weight_step(n)
+
+    @pl.when(down == 0)
+    def _():
+        @pl.loop(0, count)
+        def _(j):
+            start = pl.multiple_of((j % CHUNKS) * span + core * half + side * SHARED, 16)
+            pltpu.make_async_copy(
+                out_weight.at[pl.ds(start, taken), slab_lanes(j // CHUNKS)],
+                weight_rows(j, side * SHARED, taken, from_above),
+                right_sem.at[j],
+            ).start()
 
     for c in range(3):
         edge[pl.ds(2 * c, 2), :] = projected[c, pl.ds(rows - 16, 16), :].astype(jnp.float32)[14:, :]
-    pl.semaphore_wait(barrier, ranks - 1)
-
-    edge_copy = pltpu.make_async_remote_copy(
-        src_ref=edge,
-        dst_ref=halo,
-        send_sem=edge_sem.at[0],
-        recv_sem=edge_sem.at[1],
-        device_id=(lax.rem(rank + 1, ranks), column),
-        device_id_type=MESH,
-    )
+    pl.semaphore_wait(barrier, ranks + depth - 2)
+
+    edge_copy = remote(edge, halo, edge_sem.at[0], edge_sem.at[1], lax.rem(rank + 1, ranks), z)
     edge_copy.start()
+    weight_step(0)
     edge_copy.wait_recv()
     keep = jnp.where(rank > 0, 1.0, 0.0)
 
-    def ends_copy(owner):
-        return pltpu.make_async_remote_copy(
-            src_ref=ends.at[owner],
-            dst_ref=spread.at[rank],
-            send_sem=ends_sem.at[0],
-            recv_sem=ends_sem.at[1],
-            device_id=(owner, column),
-            device_id_type=MESH,
-        )
-
-    @pl.loop(0, ranks)
-    def _(slab):
-        first_pass(slab, keep, steps, modes, halo, projected, taps, rate, extended, queries, product, starts, ends)
-
-        @pl.when(slab == rank)
-        def _():
-            spread[rank] = ends[rank]
-
-        @pl.when(slab != rank)
-        def _():
-            ends_copy(slab).start()
-
-    def all_but_one(ref, send_sem, recv_sem):
-        return pltpu.make_async_remote_copy(
-            src_ref=ref.at[pl.ds(0, ranks - 1)],
-            dst_ref=ref.at[pl.ds(0, ranks - 1)],
-            send_sem=send_sem,
-            recv_sem=recv_sem,
-            device_id=(lax.rem(rank + 1, ranks), column),
-            device_id_type=MESH,
-        )
-
-    all_but_one(spread, ends_sem.at[0], ends_sem.at[1]).wait_recv()
+    groups = ranks // SCOPE
+
+    @pl.loop(0, groups)
+    def _(n):
+        weight_step(n + 1)
+
+        @pl.loop(0, SCOPE)
+        def _(i):
+            slab = n * SCOPE + i
+            first_pass(
+                slab, keep, steps, modes, halo, projected, taps, rate, extended, queries, product, starts, ends
+            )
+
+            @pl.when(slab == rank)
+            def _():
+                spread[rank] = ends[rank]
+
+            @pl.when(slab != rank)
+            def _():
+                remote(ends.at[slab], spread.at[rank], ends_sem.at[0], ends_sem.at[1], slab, z).start()
+
+    def all_but_one(ref, sem):
+        view = ref.at[pl.ds(0, ranks - 1)]
+        return remote(view, view, sem.at[0], sem.at[1], lax.rem(rank + 1, ranks), z)
+
+    weight_steps(groups + 1, groups + 3)
+    all_but_one(spread, ends_sem).wait_recv()
     factor = jnp.exp(rate[:, slab_lanes(rank)] * (-float(rows)))
     carried = jnp.zeros_like(factor)
     for r in range(ranks):
@@ -172,42 +288,125 @@
     @pl.loop(1, ranks)
     def _(i):
         other = lax.rem(rank + i, ranks)
-        pltpu.make_async_remote_copy(
-            src_ref=back.at[other],
-            dst_ref=before.at[rank],
-            send_sem=back_sem.at[0],
-            recv_sem=back_sem.at[1],
-            device_id=(other, column),
-            device_id_type=MESH,
-        ).start()
-
-    all_but_one(before, back_sem.at[0], back_sem.at[1]).wait_recv()
-
-    @pl.loop(0, ranks)
-    def _(slab):
-        gated[:, slab_lanes(slab)] = second_pass(
-            slab, steps, modes, queries, product, starts, before, rate, residue, bias, ordered
+        remote(back.at[other], before.at[rank], back_sem.at[0], back_sem.at[1], other, z).start()
+
+    weight_steps(groups + 3, groups + 5)
+    all_but_one(before, back_sem).wait_recv()
+
+    def rows_copy(n, slot, to_rank):
+        return remote(
+            gathered.at[n, 0], gathered.at[n, slot], rows_sem.at[0], rows_sem.at[slot], to_rank, z
         )
 
+    @pl.loop(0, groups)
+    def _(n):
+        weight_step(n + groups + 5)
+
+        @pl.loop(0, SCOPE)
+        def _(i):
+            gathered[n, 0, :, slab_lanes(i)] = second_pass(
+                n * SCOPE + i, steps, modes, queries, product, starts, before, rate, residue, bias, ordered
+            )
+
+        rows_copy(n, 1, x_up).start()
+        rows_copy(n, 2, x_down).start()
+        rows_copy(n, 3, y_out).start()
+
+    def return_copy(p, i, slot, to_rank):
+        return remote(
+            leaving.at[p, i], returned.at[p, slot], return_sem.at[0], return_sem.at[slot + PARTS * p], to_rank, z
+        )
+
+    def project(p):
+        half_part = weight.at[p, pl.ds(0, weight.shape[1] // 2)]
+        remote(half_part, half_part, sent_sem.at[3], twin_sem.at[p], twin, z).wait_recv()
+
+        def term(n):
+            block = gathered[n].reshape(BLOCKS * rows, SCOPE * LANES)
+            start = pl.multiple_of(n * SCOPE * LANES, SCOPE * LANES)
+            return jnp.dot(
+                block, weight[p, pl.ds(start, SCOPE * LANES), :], preferred_element_type=jnp.float32
+            )
+
+        total[...] = term(0)
+
+        @pl.loop(1, groups)
+        def _(n):
+            total[...] += term(n)
+
+        for i in range(3):
+            leaving[p, i] = total[pl.ds((i + 1) * rows, rows), :].astype(jnp.bfloat16)
+        returned[p, 0] = total[pl.ds(0, rows), :].astype(jnp.bfloat16)
+        return_copy(p, 0, 2, x_down).start()
+        return_copy(p, 1, 1, x_up).start()
+        return_copy(p, 2, 3, y_out).start()
+
+    def deliver(p):
+        return_copy(p, 0, 2, x_down).wait_recv()
+        return_copy(p, 1, 1, x_up).wait_recv()
+        return_copy(p, 2, 3, y_out).wait_recv()
+        for slot, block in ((0, q), (1, q + 3), (2, q + 1), (3, q + 2)):
+            for upper in range(2):
+                owner = (block % BLOCKS + BLOCKS * upper) % depth
+                view = returned.at[p, slot, :, pl.ds(upper * LANES, LANES)]
+                target = mixed.at[z, :, pl.ds(p * LANES, LANES)]
+
+                @pl.when(owner == z)
+                def _():
+                    target[...] = view[...]
+
+                @pl.when(owner != z)
+                def _():
+                    remote(view, target, mixed_sem.at[0], mixed_sem.at[1], rank, owner).start()
+
+    weight_steps(2 * groups + 5, count + SKEW * (BLOCKS + 1))
+    for slot in (1, 2, 3):
+        view = gathered.at[:, slot]
+        remote(view, view, rows_sem.at[0], rows_sem.at[slot], x_up, z).wait_recv()
+    project(0)
+    for p in range(1, PARTS):
+        project(p)
+        deliver(p - 1)
+    deliver(PARTS - 1)
+
     edge_copy.wait_send()
-    all_but_one(ends, ends_sem.at[0], ends_sem.at[1]).wait_send()
-    all_but_one(back, back_sem.at[0], back_sem.at[1]).wait_send()
+    all_but_one(ends, ends_sem).wait_send()
+    all_but_one(back, back_sem).wait_send()
+
+    def sent(view, sem):
+        remote(view, view, sem, left_sem.at[0], x_up, z).wait_send()
+
+    chain = weight.at[0, pl.ds(0, count * taken // 2)]
+    sent(chain, sent_sem.at[0])
+
+    @pl.when(down < BLOCKS - 1)
+    def _():
+        sent(chain, sent_sem.at[1])
+
+    sent(weight.at[0, pl.ds(0, count * SHARED)], sent_sem.at[2])
+    sent(weight.at[pl.ds(0, PARTS // 2)], sent_sem.at[3])
+    sent(gathered.at[:, pl.ds(0, 3)], rows_sem.at[0])
+    sent(leaving, return_sem.at[0])
+    others = mixed.at[pl.ds(0, depth - 1)]
+    remote(others, others, mixed_sem.at[0], mixed_sem.at[1], x_up, z).wait()
 
 
 def on_device(projected, short_filter, bias, residue, rate, out_weight):
     ranks = lax.axis_size("seq")
+    depth = lax.axis_size("grp")
     taken = projected[:, 0]
     rows, width = taken.shape[1:]
     modes = rate.shape[0]
     steps = rows // GROUPS
-    f32 = jnp.float32
+    f32, bf16 = jnp.float32, jnp.bfloat16
     vmem = pl.BlockSpec(memory_space=pltpu.VMEM)
     exchanged = pltpu.VMEM((ranks, modes, width // ranks), f32)
-    gated = pl.pallas_call(
-        functools.partial(front_kernel, ranks, steps, modes),
-        in_specs=[vmem] * 5,
+    dma = pltpu.SemaphoreType.DMA
+    return pl.pallas_call(
+        functools.partial(block_kernel, ranks, steps, modes),
+        in_specs=[vmem] * 5 + [pl.BlockSpec(memory_space=pl.ANY)],
         out_specs=vmem,
-        out_shape=jax.ShapeDtypeStruct((rows, width), jnp.bfloat16),
+        out_shape=jax.ShapeDtypeStruct((depth, rows, out_weight.shape[1]), bf16),
         scratch_shapes=[
             pltpu.VMEM((3, rows + 8, LANES), f32),
             pltpu.VMEM((rows, LANES), f32),
@@ -220,20 +419,27 @@
             exchanged,
             exchanged,
             exchanged,
-            pltpu.SemaphoreType.DMA((2,)),
-            pltpu.SemaphoreType.DMA((2,)),
-            pltpu.SemaphoreType.DMA((2,)),
+            pltpu.VMEM((PARTS, width, 2 * LANES), bf16),
+            pltpu.VMEM((ranks // SCOPE, BLOCKS, rows, SCOPE * LANES), bf16),
+            pltpu.VMEM((BLOCKS * rows, 2 * LANES), f32),
+            pltpu.VMEM((PARTS, 3, rows, 2 * LANES), bf16),
+            pltpu.VMEM((PARTS, BLOCKS, rows, 2 * LANES), bf16),
+            dma((2,)),
+            dma((2,)),
+            dma((2,)),
+            dma((PARTS * CHUNKS,)),
+            dma((PARTS * CHUNKS,)),
+            dma((PARTS * CHUNKS,)),
+            dma((PARTS,)),
+            dma((4,)),
+            dma((4,)),
+            dma((4 * PARTS,)),
+            dma((2,)),
         ],
         compiler_params=pltpu.CompilerParams(
             collective_id=0, has_side_effects=True, vmem_limit_bytes=48 * MIB
         ),
-    )(taken, short_filter, rate, residue, bias[None])
-    return jnp.einsum(
-        "srd,de->sre",
-        lax.all_gather(gated[None], "grp", axis=0, tiled=True),
-        out_weight,
-        preferred_element_type=jnp.float32,
-    ).astype(jnp.bfloat16)
+    )(taken, short_filter, rate, residue, bias[None], out_weight)
 
 
 def solution(mesh):

time: 160 us -> 112 us (0.70)
  waiting for transfers between devices: 96.2 us -> 0 us
  Pallas kernels: 33.8 us -> 105 us
  between operations: 13.4 us -> 0.01 us
  matrix products: 10 us -> 0 us
    all_gather x1 -> x0, waiting for transfers between devices: 96.1 us -> none  [on_device(): lax.all_gather(gated[None], 'grp', axis=0, tiled=True)]
    pallas_call x1, Pallas kernels: 33.8 us -> 105 us  [on_device(): pl.pallas_call(functools.partial(block_kernel, ranks, steps, modes), in_s...]
    dot_general x1 -> x0, matrix products: 10 us -> none  [on_device(): jnp.einsum('srd,de->sre', lax.all_gather(gated[None], 'grp', axis=0, tile...]
    unnamed x10 -> x11, local copies, waits for them, and re-layouts: 5.43 us -> 6.4 us
  transfers between devices with their start and end apart: 1 -> 0, of which waited for: 1 -> 0; matrix products, arithmetic and copies ran while one was open for 0% -> 0% of each run, Pallas kernels for 0% -> 0%
where the time goes in v3:
time: 112 us; the launch traced here: 111 us
  Pallas kernels  105 us (94%)
  local copies, waits for them, and re-layouts  6.4 us (6%)
    pallas_call x1, Pallas kernels, on_device(): pl.pallas_call(functools.partial(block_kernel, ranks, steps, modes), in_s...  105 us
    unnamed x11, local copies, waits for them, and re-layouts  6.4 us

profile of v3, /device:TPU:4, one launch (start us, length us, event | category | flops | bytes accessed | tf_op | source)
XLA Modules:
  0.0 111.4 jit_solution(14908463408519681675)
XLA Ops:
  0.0 0.0 copy-start
  0.0 1.9 %copy-done = bf16[3,1,128,4096]{3,2,1,0:T(8,128)(2,1)S(1)} copy-done((bf16[3,1,128,4096]{3,2,1,0:T(8,128)(2,1)S(1)}, bf16[3,1,128,4096]{3,2,1,0:T(8,128)(2,1)}, u32[]{:S(2)}) %copy-start) | copy-done | bytes 3145752
  1.9 0.0 copy-start.1
  1.9 0.9 copy-done.1
  2.8 0.0 copy-start.2
  2.8 0.9 copy-done.2
  3.8 0.0 copy-start.3
  3.8 0.9 copy-done.3
  4.7 0.0 copy-start.4
  4.7 0.7 copy-done.4
  5.4 104.9 %shard_map.64 = bf16[8,128,512]{2,1,0:T(8,128)(2,1)S(1)} custom-call(bf16[3,128,4096]{2,1,0:T(8,128)(2,1)S(1)} %bitcast.2, f32[3,3,4096]{2,1,0:T(4,128)S(1)} %copy-done.3, f32[16,4096]{1,0:T(8,128)S(1)} %copy-done.1, f32[16,4096]{1,0:T(8,128)S(1)} %copy-done.2, f32[1,4096]{1,0:T(1,128)S(1)} %bitcast.3, bf16[4096,512]{1,0:T(8,128)(2,1)} %out_weight.1), custom_call_target="tpu_custom_call" | custom-call | tf_op jit(solution)/shard_map/pallas_call | solution.py:405
  110.4 1.0 copy.8
Async XLA Ops:
  0.0 1.9 %copy-start = (bf16[3,1,128,4096]{3,2,1,0:T(8,128)(2,1)S(1)}, bf16[3,1,128,4096]{3,2,1,0:T(8,128)(2,1)}, u32[]{:S(2)}) copy-start(bf16[3,1,128,4096]{3,2,1,0:T(8,128)(2,1)} %param.6) | copy-start | bytes 9437188
  1.9 0.9 copy-start.1
  2.8 0.9 copy-start.2
  3.8 0.9 copy-start.3
  4.7 0.7 copy-start.4

commit v4 on v3

v4 whole, which is shorter than its diff:
```python
import functools

import jax
import jax.numpy as jnp
from jax import lax
from jax.experimental import pallas as pl
from jax.experimental.pallas import tpu as pltpu
from jax.sharding import PartitionSpec as P

LANES = 128
GROUPS = 8
MIB = 1024 * 1024


MESH = pl.DeviceIdType.MESH


def slab_lanes(slab):
    return pl.ds(pl.multiple_of(slab * LANES, LANES), LANES)


def wide(row):
    return jnp.broadcast_to(row, (GROUPS, LANES))


def first_pass(slab, keep, steps, modes, halo, projected, taps, rate, extended, queries, product, starts, ends):
    lanes = slab_lanes(slab)
    bands = starts.shape[0]
    count = steps * GROUPS
    for c in range(3):
        extended[c, pl.ds(6, 2), :] = halo[pl.ds(2 * c, 2), lanes] * keep
        extended[c, pl.ds(8, bands * count), :] = projected[c, :, lanes].astype(jnp.float32)
    speed = [wide(rate[pl.ds(m, 1), lanes]) for m in range(modes)]
    decay = [jnp.exp(-speed[m]) for m in range(modes)]
    tap = [[wide(taps[c, pl.ds(j, 1), lanes]) for j in range(3)] for c in range(3)]
    row = lax.broadcasted_iota(jnp.int32, (GROUPS, LANES), 0)
    last = None
    for band in range(bands):
        first = 8 + band * count
        held = [[extended[c, pl.ds(first - j, GROUPS, stride=steps), :] for j in (2, 1)] for c in range(3)]
        initial = [None if last is None else jnp.where(row == 0, last[m], 0.0) for m in range(modes)]
        state = list(initial)
        for i in range(steps):
            featured = []
            for c in range(3):
                now = extended[c, pl.ds(first + i, GROUPS, stride=steps), :]
                featured.append(tap[c][0] * now + tap[c][1] * held[c][1] + tap[c][2] * held[c][0])
                held[c] = [held[c][1], now]
            x = featured[1] * featured[2]
            queries[band * steps + i, :, lanes] = featured[0]
            product[band * steps + i, :, lanes] = x
            for m in range(modes):
                state[m] = x if state[m] is None else decay[m] * state[m] + x
        last = []
        for m in range(modes):
            here = state[m]
            for distance in (1, 2, 4):
                factor = jnp.where(row >= distance, jnp.exp(speed[m] * (-float(steps * distance))), 0.0)
                here = here + factor * pltpu.roll(here, distance, 0)
            ahead = 0.0 if initial[m] is None else initial[m]
            starts[band, m, :, lanes] = jnp.where(row >= 1, pltpu.roll(here, 1, 0), ahead)
            last.append(wide(here[GROUPS - 1 :, :]))
            if band == bands - 1:
                ends[slab, pl.ds(m, 1), :] = here[GROUPS - 1 :, :]


def second_pass(band, slab, steps, modes, queries, product, starts, before, rate, residue, bias, ordered):
    lanes = slab_lanes(slab)
    row = lax.broadcasted_iota(jnp.int32, (GROUPS, LANES), 0)
    position = ((row + band * GROUPS) * steps).astype(jnp.float32)
    decay, weight, state = [], [], []
    for m in range(modes):
        speed = wide(rate[pl.ds(m, 1), lanes])
        decay.append(jnp.exp(-speed))
        weight.append(wide(residue[pl.ds(m, 1), lanes]))
        carried = jnp.exp(-speed * position) * wide(before[slab, pl.ds(m, 1), :])
        state.append(starts[band, m, :, lanes] + carried)
    skip = wide(bias[pl.ds(0, 1), lanes])
    for i in range(steps):
        x = product[band * steps + i, :, lanes]
        total = skip * x
        for m in range(modes):
            state[m] = decay[m] * state[m] + x
            total = total + weight[m] * state[m]
        ordered[pl.ds(i, GROUPS, stride=steps), :] = queries[band * steps + i, :, lanes] * total
    return ordered[...].astype(jnp.bfloat16)


BANDS = 2
BLOCKS = 4
PARTS = 4
CHUNKS = 8
SHARED = 96
SKEW = 4
SCOPE = 4
WAY = -1
PACE = 1
AHEAD = 5
LAG = 2
ORDER = ((44, 0, 0), (44, 0, 1), (46, 0, 2), (48, 1, 0), (50, 1, 1), (52, 1, 2), (52, 0, 3), (52, 1, 3))


def block_kernel(
    ranks,
    steps,
    modes,
    projected_in,
    taps_in,
    rate_in,
    residue_in,
    bias_in,
    out_weight,
    mixed,
    projected,
    taps,
    rate,
    residue,
    bias,
    last,
    extended,
    ordered,
    queries,
    product,
    starts,
    edge,
    halo,
    ends,
    spread,
    back,
    before,
    weight,
    gathered,
    total,
    leaving,
    returned,
    edge_sem,
    ends_sem,
    back_sem,
    left_sem,
    right_sem,
    swap_sem,
    twin_sem,
    sent_sem,
    rows_sem,
    return_sem,
    mixed_sem,
    input_sem,
    rows_in_sem,
):
    rank = lax.axis_index("seq")
    z = lax.axis_index("grp")
    depth = mixed.shape[0]
    rows = projected.shape[1]
    band_rows = steps * GROUPS
    x, y, core = rank // 8, (rank // 2) % 4, rank % 2
    side = y % 2
    q = (x + 2 * (y // 2)) % BLOCKS

    def at(px, py, pcore):
        return (px % 4) * 8 + (py % 4) * 2 + pcore

    x_up, x_down = at(x + 1, y, core), at(x + 3, y, core)
    y_out = at(x, y + 3 + 2 * side, core)
    y_pair = at(x, y + 1 - 2 * side, core)
    twin = at(x, y, 1 - core)

    def remote(source, target, send_sem, recv_sem, to_rank, to_z):
        return pltpu.make_async_remote_copy(
            src_ref=source,
            dst_ref=target,
            send_sem=send_sem,
            recv_sem=recv_sem,
            device_id=(to_rank, to_z),
            device_id_type=MESH,
        )

    groups = ranks // SCOPE
    wide_lanes = SCOPE * LANES

    last_in = pltpu.make_async_copy(projected_in.at[:, pl.ds(rows - 16, 16)], last, input_sem.at[0])
    last_in.start()
    small = [
        pltpu.make_async_copy(source, target, input_sem.at[1 + i])
        for i, (source, target) in enumerate(
            ((taps_in, taps), (rate_in, rate), (residue_in, residue), (bias_in, bias))
        )
    ]
    for copy in small:
        copy.start()

    def rows_in(n):
        lanes = pl.ds(pl.multiple_of(n * wide_lanes, wide_lanes), wide_lanes)
        return pltpu.make_async_copy(
            projected_in.at[:, :, lanes], projected.at[:, :, lanes], rows_in_sem.at[n]
        )

    @pl.loop(0, groups)
    def _(n):
        rows_in(n).start()

    barrier = pltpu.get_barrier_semaphore()

    @pl.loop(1, ranks)
    def _(i):
        pl.semaphore_signal(barrier, inc=1, device_id=(lax.rem(rank + i, ranks), z), device_id_type=MESH)

    @pl.loop(1, depth)
    def _(i):
        pl.semaphore_signal(barrier, inc=1, device_id=(rank, lax.rem(z + i, depth)), device_id_type=MESH)

    up = (WAY * (z - q) + depth) % BLOCKS
    down = (WAY * (q - z) + depth) % BLOCKS
    from_above = ((z + WAY * down + 2 * depth - q) % depth) // BLOCKS
    from_below = 1 - from_above
    span = weight.shape[1] // CHUNKS
    half = span // 2
    taken = half - SHARED
    count = PARTS * CHUNKS

    def weight_rows(j, offset, size, block=None):
        start = pl.multiple_of((j % CHUNKS) * span + core * half + offset, 16)
        columns = pl.ds(0, 2 * LANES) if block is None else slab_lanes(block)
        return weight.at[j // CHUNKS, pl.ds(start, size), columns]

    def moving(j, block, send_sem, recv_sem, to_z):
        view = weight_rows(j, side * SHARED, taken, block)
        return remote(view, view, send_sem, recv_sem.at[j], rank, to_z % depth)

    def upward(j, block):
        return moving(j, block, sent_sem.at[0], left_sem, z + depth + WAY)

    def downward(j, block):
        return moving(j, block, sent_sem.at[1], right_sem, z + depth - WAY)

    def swap(j, block):
        view = weight_rows(j, side * taken, SHARED, block)
        return remote(view, view, sent_sem.at[2], swap_sem.at[j], y_pair, z)

    def weight_step(n):
        j = n - SKEW * down

        @pl.when((j >= 0) & (j < count))
        def _():
            downward(j, from_above).wait_recv()

            @pl.when(down < BLOCKS - 1)
            def _():
                downward(j, from_above).start()

            @pl.when(up == 0)
            def _():
                upward(j, from_above).start()

            swap(j, from_above).start()

        k = n - SKEW * jnp.where(up == 0, BLOCKS, up)

        @pl.when((k >= 0) & (k < count))
        def _():
            upward(k, from_below).wait_recv()

            @pl.when(up > 0)
            def _():
                upward(k, from_below).start()

            swap(k, from_below).start()

        whole = n - SKEW * (BLOCKS + 1)

        @pl.when((whole >= 0) & (whole < count))
        def _():
            other = weight_rows(whole, (1 - side) * taken, SHARED)
            remote(other, other, sent_sem.at[2], swap_sem.at[whole], y_pair, z).wait_recv()
            view = weight_rows(whole, 0, half)
            remote(view, view, sent_sem.at[3], twin_sem.at[whole // CHUNKS], twin, z).start()

    def weight_steps(first, last):
        @pl.loop(first, last)
        def _(n):
            weight_step(n)

    @pl.when(down == 0)
    def _():
        @pl.loop(0, count)
        def _(j):
            start = pl.multiple_of((j % CHUNKS) * span + core * half + side * SHARED, 16)
            pltpu.make_async_copy(
                out_weight.at[pl.ds(start, taken), slab_lanes(j // CHUNKS)],
                weight_rows(j, side * SHARED, taken, from_above),
                right_sem.at[j],
            ).start()

    last_in.wait()
    for c in range(3):
        edge[pl.ds(2 * c, 2), :] = last[c].astype(jnp.float32)[14:, :]
    pl.semaphore_wait(barrier, ranks + depth - 2)

    edge_copy = remote(edge, halo, edge_sem.at[0], edge_sem.at[1], lax.rem(rank + 1, ranks), z)
    edge_copy.start()
    weight_step(0)
    for copy in small:
        copy.wait()
    edge_copy.wait_recv()
    keep = jnp.where(rank > 0, 1.0, 0.0)

    def all_but_one(ref, send_sem, recv_sem):
        view = ref.at[pl.ds(0, ranks - 1)]
        return remote(view, view, send_sem, recv_sem, lax.rem(rank + 1, ranks), z)

    def first_group(n):
        rows_in(n).wait()

        @pl.loop(0, SCOPE)
        def _(i):
            slab = n * SCOPE + (i + rank) % SCOPE
            first_pass(
                slab, keep, steps, modes, halo, projected, taps, rate, extended, queries, product, starts, ends
            )

            @pl.when(slab == rank)
            def _():
                spread[rank] = ends[rank]

            @pl.when(slab != rank)
            def _():
                remote(ends.at[slab], spread.at[rank], ends_sem.at[0], ends_sem.at[1], slab, z).start()

    def scan():
        all_but_one(spread, ends_sem.at[0], ends_sem.at[1]).wait_recv()
        factor = jnp.exp(rate[:, slab_lanes(rank)] * (-float(rows)))
        carried = jnp.zeros_like(factor)
        for r in range(ranks):
            back[r] = carried
            carried = factor * carried + spread[r]
        arrival = back_sem.at[1 + rank // SCOPE]
        pltpu.make_async_copy(back.at[rank], before.at[rank], arrival).start()

        @pl.loop(1, ranks)
        def _(i):
            other = lax.rem(rank + i, ranks)
            remote(back.at[other], before.at[rank], back_sem.at[0], arrival, other, z).start()

    def rows_copy(band, n, slot, to_rank):
        return remote(
            gathered.at[band, n, 0],
            gathered.at[band, n, slot],
            rows_sem.at[0],
            rows_sem.at[3 * band + slot],
            to_rank,
            z,
        )

    def second_group(band, n):
        if band == 0:
            view = before.at[pl.ds(n * SCOPE, SCOPE)]
            remote(view, view, back_sem.at[0], back_sem.at[1 + n], x_up, z).wait_recv()

        @pl.loop(0, SCOPE)
        def _(i):
            gathered[band, n, 0, :, slab_lanes(i)] = second_pass(
                band, n * SCOPE + i, steps, modes, queries, product, starts, before, rate, residue, bias, ordered
            )

        rows_copy(band, n, 1, x_up).start()
        rows_copy(band, n, 2, x_down).start()
        rows_copy(band, n, 3, y_out).start()

    @pl.loop(0, groups)
    def _(n):
        for i in range(PACE):
            weight_step(n * PACE + 1 + i)
        first_group((n + rank // SCOPE) % groups)

    step = 1 + PACE * groups
    weight_steps(step, step + AHEAD)
    scan()
    weight_steps(step + AHEAD, step + 2 * AHEAD)

    step = step + 2 * AHEAD
    for band in range(BANDS):

        @pl.loop(0, groups)
        def _(n):
            for i in range(PACE):
                weight_step(n * PACE + step + i)
            second_group(band, n)

        step += PACE * groups

    def return_copy(band, p, i, slot, to_rank):
        return remote(
            leaving.at[band, p, i],
            returned.at[band, p, slot],
            return_sem.at[0],
            return_sem.at[slot + 3 * (p + PARTS * band)],
            to_rank,
            z,
        )

    def project(band, p):
        def term(n):
            block = gathered[band, n].reshape(BLOCKS * band_rows, wide_lanes)
            start = pl.multiple_of(n * wide_lanes, wide_lanes)
            return jnp.dot(block, weight[p, pl.ds(start, wide_lanes), :], preferred_element_type=jnp.float32)

        total[...] = term(0)

        @pl.loop(1, groups)
        def _(n):
            total[...] += term(n)

        for i in range(3):
            leaving[band, p, i] = total[pl.ds((i + 1) * band_rows, band_rows), :].astype(jnp.bfloat16)
        returned[band, p, 0] = total[pl.ds(0, band_rows), :].astype(jnp.bfloat16)
        return_copy(band, p, 0, 2, x_down).start()
        return_copy(band, p, 1, 1, x_up).start()
        return_copy(band, p, 2, 3, y_out).start()

    def deliver(band, p):
        return_copy(band, p, 0, 2, x_down).wait_recv()
        return_copy(band, p, 1, 1, x_up).wait_recv()
        return_copy(band, p, 2, 3, y_out).wait_recv()
        for slot, block in ((0, q), (1, q + 3), (2, q + 1), (3, q + 2)):
            for upper in range(2):
                owner = (block % BLOCKS + BLOCKS * upper) % depth
                view = returned.at[band, p, slot, :, pl.ds(upper * LANES, LANES)]
                target = mixed.at[z, pl.ds(band * band_rows, band_rows), pl.ds(p * LANES, LANES)]

                @pl.when(owner == z)
                def _():
                    target[...] = view[...]

                @pl.when(owner != z)
                def _():
                    remote(view, target, mixed_sem.at[0], mixed_sem.at[1], rank, owner).start()

    waiting = []
    bands_here, parts_here = set(), set()
    for until, band, p in ORDER:
        if until > step:
            weight_steps(step, until)
            step = until
        if band not in bands_here:
            bands_here.add(band)
            for slot in (1, 2, 3):
                view = gathered.at[band, :, slot]
                remote(view, view, rows_sem.at[0], rows_sem.at[3 * band + slot], x_up, z).wait_recv()
        if p not in parts_here:
            parts_here.add(p)
            half_part = weight.at[p, pl.ds(0, weight.shape[1] // 2)]
            remote(half_part, half_part, sent_sem.at[3], twin_sem.at[p], twin, z).wait_recv()
        project(band, p)
        waiting.append((band, p))
        if len(waiting) > LAG:
            deliver(*waiting.pop(0))
    for item in waiting:
        deliver(*item)

    edge_copy.wait_send()
    all_but_one(ends, ends_sem.at[0], ends_sem.at[1]).wait_send()
    all_but_one(back, back_sem.at[0], back_sem.at[1]).wait_send()

    def sent(view, sem):
        remote(view, view, sem, left_sem.at[0], x_up, z).wait_send()

    chain = weight.at[0, pl.ds(0, count * taken // 2)]
    sent(chain, sent_sem.at[0])

    @pl.when(down < BLOCKS - 1)
    def _():
        sent(chain, sent_sem.at[1])

    sent(weight.at[0, pl.ds(0, count * SHARED)], sent_sem.at[2])
    sent(weight.at[pl.ds(0, PARTS // 2)], sent_sem.at[3])
    sent(gathered.at[:, :, pl.ds(0, 3)], rows_sem.at[0])
    sent(leaving, return_sem.at[0])
    others = mixed.at[pl.ds(0, depth - 1)]
    remote(others, others, mixed_sem.at[0], mixed_sem.at[1], x_up, z).wait()


def on_device(projected, short_filter, bias, residue, rate, out_weight):
    ranks = lax.axis_size("seq")
    depth = lax.axis_size("grp")
    taken = projected[:, 0]
    rows, width = taken.shape[1:]
    modes = rate.shape[0]
    steps = rows // (GROUPS * BANDS)
    f32, bf16 = jnp.float32, jnp.bfloat16
    vmem = pl.BlockSpec(memory_space=pltpu.VMEM)
    exchanged = pltpu.VMEM((ranks, modes, width // ranks), f32)
    dma = pltpu.SemaphoreType.DMA
    return pl.pallas_call(
        functools.partial(block_kernel, ranks, steps, modes),
        in_specs=[pl.BlockSpec(memory_space=pl.ANY)] * 6,
        out_specs=vmem,
        out_shape=jax.ShapeDtypeStruct((depth, rows, out_weight.shape[1]), bf16),
        scratch_shapes=[
            pltpu.VMEM(taken.shape, bf16),
            pltpu.VMEM(short_filter.shape, f32),
            pltpu.VMEM(rate.shape, f32),
            pltpu.VMEM(residue.shape, f32),
            pltpu.VMEM((1, width), f32),
            pltpu.VMEM((3, 16, width), bf16),
            pltpu.VMEM((3, rows + 8, LANES), f32),
            pltpu.VMEM((steps * GROUPS, LANES), f32),
            pltpu.VMEM((BANDS * steps, GROUPS, width), f32),
            pltpu.VMEM((BANDS * steps, GROUPS, width), f32),
            pltpu.VMEM((BANDS, modes, GROUPS, width), f32),
            pltpu.VMEM((8, width), f32),
            pltpu.VMEM((8, width), f32),
            exchanged,
            exchanged,
            exchanged,
            exchanged,
            pltpu.VMEM((PARTS, width, 2 * LANES), bf16),
            pltpu.VMEM((BANDS, ranks // SCOPE, BLOCKS, rows // BANDS, SCOPE * LANES), bf16),
            pltpu.VMEM((BLOCKS * rows // BANDS, 2 * LANES), f32),
            pltpu.VMEM((BANDS, PARTS, 3, rows // BANDS, 2 * LANES), bf16),
            pltpu.VMEM((BANDS, PARTS, BLOCKS, rows // BANDS, 2 * LANES), bf16),
            dma((2,)),
            dma((2,)),
            dma((1 + ranks // SCOPE,)),
            dma((PARTS * CHUNKS,)),
            dma((PARTS * CHUNKS,)),
            dma((PARTS * CHUNKS,)),
            dma((PARTS,)),
            dma((4,)),
            dma((1 + 3 * BANDS,)),
            dma((1 + 3 * BANDS * PARTS,)),
            dma((2,)),
            dma((5,)),
            dma((ranks // SCOPE,)),
        ],
        compiler_params=pltpu.CompilerParams(
            collective_id=0, has_side_effects=True, vmem_limit_bytes=48 * MIB
        ),
    )(taken, short_filter, rate, residue, bias[None], out_weight)


def solution(mesh):
    placed = (P(None, "grp", "seq", None), P(), P(), P(), P(), P(None, "grp"))
    return jax.shard_map(
        on_device, mesh=mesh, in_specs=placed, out_specs=P(None, "seq", "grp"), check_vma=False
    )
```

time: 112 us -> 93.2 us (0.83)
  Pallas kernels: 105 us -> 85.8 us
    pallas_call x1, Pallas kernels: 105 us -> 85.8 us  [on_device(): pl.pallas_call(functools.partial(block_kernel, ranks, steps, modes), in_s...]
where the time goes in v4:
time: 93.2 us; the launch traced here: 92.2 us
  Pallas kernels  85.8 us (92%)
  local copies, waits for them, and re-layouts  6.4 us (7%)
    pallas_call x1, Pallas kernels, on_device(): pl.pallas_call(functools.partial(block_kernel, ranks, steps, modes), in_s...  85.8 us
    unnamed x11, local copies, waits for them, and re-layouts  6.4 us

profile of v4, /device:TPU:4, one launch (start us, length us, event | category | flops | bytes accessed | tf_op | source)
XLA Modules:
  0.0 92.2 jit_solution(2884808522846358222)
XLA Ops:
  0.0 0.0 copy-start
  0.0 1.9 %copy-done = bf16[3,1,128,4096]{3,2,1,0:T(8,128)(2,1)S(1)} copy-done((bf16[3,1,128,4096]{3,2,1,0:T(8,128)(2,1)S(1)}, bf16[3,1,128,4096]{3,2,1,0:T(8,128)(2,1)}, u32[]{:S(2)}) %copy-start) | copy-done | bytes 3145752
  1.9 0.0 copy-start.1
  1.9 0.9 %copy-done.1 = f32[16,4096]{1,0:T(8,128)S(1)} copy-done((f32[16,4096]{1,0:T(8,128)S(1)}, f32[16,4096]{1,0:T(8,128)}, u32[]{:S(2)}) %copy-start.1) | copy-done | bytes 262168
  2.8 0.0 copy-start.2
  2.8 0.9 %copy-done.2 = f32[16,4096]{1,0:T(8,128)S(1)} copy-done((f32[16,4096]{1,0:T(8,128)S(1)}, f32[16,4096]{1,0:T(8,128)}, u32[]{:S(2)}) %copy-start.2) | copy-done | bytes 262168
  3.8 0.0 copy-start.3
  3.8 0.9 %copy-done.3 = f32[3,3,4096]{2,1,0:T(4,128)S(1)} copy-done((f32[3,3,4096]{2,1,0:T(4,128)S(1)}, f32[3,3,4096]{2,1,0:T(4,128)}, u32[]{:S(2)}) %copy-start.3) | copy-done | bytes 147480
  4.7 0.0 copy-start.4
  4.7 0.7 copy-done.4
  5.4 85.8 %shard_map.64 = bf16[8,128,512]{2,1,0:T(8,128)(2,1)S(1)} custom-call(bf16[3,128,4096]{2,1,0:T(8,128)(2,1)S(1)} %bitcast.2, f32[3,3,4096]{2,1,0:T(4,128)S(1)} %copy-done.3, f32[16,4096]{1,0:T(8,128)S(1)} %copy-done.1, f32[16,4096]{1,0:T(8,128)S(1)} %copy-done.2, f32[1,4096]{1,0:T(1,128)S(1)} %bitcast.3, bf16[4096,512]{1,0:T(8,128)(2,1)} %out_weight.1), custom_call_target="tpu_custom_call" | custom-call | tf_op jit(solution)/shard_map/pallas_call | solution.py:492
  91.2 1.0 %copy.8 = bf16[8,128,512]{2,1,0:T(8,128)(2,1)} copy(bf16[8,128,512]{2,1,0:T(8,128)(2,1)S(1)} %shard_map.64) | data formatting | bytes 2097152
Async XLA Ops:
  0.0 1.9 %copy-start = (bf16[3,1,128,4096]{3,2,1,0:T(8,128)(2,1)S(1)}, bf16[3,1,128,4096]{3,2,1,0:T(8,128)(2,1)}, u32[]{:S(2)}) copy-start(bf16[3,1,128,4096]{3,2,1,0:T(8,128)(2,1)} %param.6) | copy-start | bytes 9437188
  1.9 0.9 %copy-start.1 = (f32[16,4096]{1,0:T(8,128)S(1)}, f32[16,4096]{1,0:T(8,128)}, u32[]{:S(2)}) copy-start(f32[16,4096]{1,0:T(8,128)} %rate_in.1) | copy-start | bytes 786436
  2.8 0.9 %copy-start.2 = (f32[16,4096]{1,0:T(8,128)S(1)}, f32[16,4096]{1,0:T(8,128)}, u32[]{:S(2)}) copy-start(f32[16,4096]{1,0:T(8,128)} %residue_in.1) | copy-start | bytes 786436
  3.8 0.9 %copy-start.3 = (f32[3,3,4096]{2,1,0:T(4,128)S(1)}, f32[3,3,4096]{2,1,0:T(4,128)}, u32[]{:S(2)}) copy-start(f32[3,3,4096]{2,1,0:T(4,128)} %taps_in.1) | copy-start | bytes 442372
  4.7 0.7 copy-start.4

commit v5 on v4

--- a/solution.py
+++ b/solution.py
@@ -97,7 +97,7 @@
 PACE = 1
 AHEAD = 5
 LAG = 2
-ORDER = ((44, 0, 0), (44, 0, 1), (46, 0, 2), (48, 1, 0), (50, 1, 1), (52, 1, 2), (52, 0, 3), (52, 1, 3))
+ORDER = ((40, 0, 0), (42, 0, 1), (44, 0, 2), (48, 1, 0), (50, 1, 1), (52, 1, 2), (52, 0, 3), (52, 1, 3))
 
 
 def block_kernel(
@@ -532,7 +532,7 @@
             dma((ranks // SCOPE,)),
         ],
         compiler_params=pltpu.CompilerParams(
-            collective_id=0, has_side_effects=True, vmem_limit_bytes=48 * MIB
+            collective_id=0, has_side_effects=True, vmem_limit_bytes=62 * MIB
         ),
     )(taken, short_filter, rate, residue, bias[None], out_weight)
 

time: 93.2 us -> 88.5 us (0.950)
  local copies, waits for them, and re-layouts: 6.4 us -> 2.26 us
    unnamed x11 -> x1, local copies, waits for them, and re-layouts: 6.4 us -> 2.26 us
where the time goes in v5:
time: 88.5 us; the launch traced here: 87.5 us
  Pallas kernels  85.3 us (96%)
  local copies, waits for them, and re-layouts  2.26 us (3%)
    pallas_call x1, Pallas kernels, on_device(): pl.pallas_call(functools.partial(block_kernel, ranks, steps, modes), in_s...  85.3 us
    unnamed x1, local copies, waits for them, and re-layouts  2.26 us

profile of v5, /device:TPU:4, one launch (start us, length us, event | category | flops | bytes accessed | tf_op | source)
XLA Modules:
  0.0 87.5 jit_solution(6938389219572971066)
XLA Ops:
  0.0 85.3 %shard_map.64 = bf16[8,128,512]{2,1,0:T(8,128)(2,1)} custom-call(bf16[3,128,4096]{2,1,0:T(8,128)(2,1)} %bitcast.2, f32[3,3,4096]{2,1,0:T(4,128)} %taps_in.1, f32[16,4096]{1,0:T(8,128)} %rate_in.1, f32[16,4096]{1,0:T(8,128)} %residue_in.1, f32[1,4096]{1,0:T(1,128)} %bitcast.3, bf16[4096,512]{1,0:T(8,128)(2,1)} %out_weight.1), custom_call_target="tpu_custom_call" | custom-call | tf_op jit(solution)/shard_map/pallas_call | solution.py:492
  85.3 2.3 %copy.8 = bf16[8,128,512]{2,1,0:T(8,128)(2,1)} copy(bf16[8,128,512]{2,1,0:T(8,128)(2,1)} %shard_map.64) | data formatting | bytes 2097152

commit v6 on v5

--- a/solution.py
+++ b/solution.py
@@ -23,57 +23,63 @@
     return jnp.broadcast_to(row, (GROUPS, LANES))
 
 
-def first_pass(slab, keep, steps, modes, halo, projected, taps, rate, extended, queries, product, starts, ends):
+def first_pass(band, slab, keep, steps, modes, halo, projected, taps, rate, extended, queries, product, starts, middle, ends):
     lanes = slab_lanes(slab)
-    bands = starts.shape[0]
     count = steps * GROUPS
+    first = 8 + band * count
+    ahead = 16 * band
     for c in range(3):
-        extended[c, pl.ds(6, 2), :] = halo[pl.ds(2 * c, 2), lanes] * keep
-        extended[c, pl.ds(8, bands * count), :] = projected[c, :, lanes].astype(jnp.float32)
+        if band == 0:
+            extended[c, pl.ds(6, 2), :] = halo[pl.ds(2 * c, 2), lanes] * keep
+        extended[c, pl.ds(first - ahead, count + ahead), :] = projected[
+            c, pl.ds(band * count - ahead, count + ahead), lanes
+        ].astype(jnp.float32)
     speed = [wide(rate[pl.ds(m, 1), lanes]) for m in range(modes)]
     decay = [jnp.exp(-speed[m]) for m in range(modes)]
     tap = [[wide(taps[c, pl.ds(j, 1), lanes]) for j in range(3)] for c in range(3)]
     row = lax.broadcasted_iota(jnp.int32, (GROUPS, LANES), 0)
-    last = None
-    for band in range(bands):
-        first = 8 + band * count
-        held = [[extended[c, pl.ds(first - j, GROUPS, stride=steps), :] for j in (2, 1)] for c in range(3)]
-        initial = [None if last is None else jnp.where(row == 0, last[m], 0.0) for m in range(modes)]
-        state = list(initial)
-        for i in range(steps):
-            featured = []
-            for c in range(3):
-                now = extended[c, pl.ds(first + i, GROUPS, stride=steps), :]
-                featured.append(tap[c][0] * now + tap[c][1] * held[c][1] + tap[c][2] * held[c][0])
-                held[c] = [held[c][1], now]
-            x = featured[1] * featured[2]
-            queries[band * steps + i, :, lanes] = featured[0]
-            product[band * steps + i, :, lanes] = x
-            for m in range(modes):
-                state[m] = x if state[m] is None else decay[m] * state[m] + x
-        last = []
+    held = [[extended[c, pl.ds(first - j, GROUPS, stride=steps), :] for j in (2, 1)] for c in range(3)]
+    state = [None] * modes
+    for i in range(steps):
+        featured = []
+        for c in range(3):
+            now = extended[c, pl.ds(first + i, GROUPS, stride=steps), :]
+            featured.append(tap[c][0] * now + tap[c][1] * held[c][1] + tap[c][2] * held[c][0])
+            held[c] = [held[c][1], now]
+        x = featured[1] * featured[2]
+        queries[band * steps + i, :, lanes] = featured[0]
+        product[band * steps + i, :, lanes] = x
         for m in range(modes):
-            here = state[m]
-            for distance in (1, 2, 4):
-                factor = jnp.where(row >= distance, jnp.exp(speed[m] * (-float(steps * distance))), 0.0)
-                here = here + factor * pltpu.roll(here, distance, 0)
-            ahead = 0.0 if initial[m] is None else initial[m]
-            starts[band, m, :, lanes] = jnp.where(row >= 1, pltpu.roll(here, 1, 0), ahead)
-            last.append(wide(here[GROUPS - 1 :, :]))
-            if band == bands - 1:
-                ends[slab, pl.ds(m, 1), :] = here[GROUPS - 1 :, :]
-
-
-def second_pass(band, slab, steps, modes, queries, product, starts, before, rate, residue, bias, ordered):
+            state[m] = x if i == 0 else decay[m] * state[m] + x
+    for m in range(modes):
+        here = state[m]
+        for distance in (1, 2, 4):
+            factor = jnp.where(row >= distance, jnp.exp(speed[m] * (-float(steps * distance))), 0.0)
+            here = here + factor * pltpu.roll(here, distance, 0)
+        starts[band, m, :, lanes] = jnp.where(row >= 1, pltpu.roll(here, 1, 0), 0.0)
+        last = here[GROUPS - 1 :, :]
+        if band:
+            ends[slab, pl.ds(m, 1), :] = last
+        else:
+            middle[slab, pl.ds(m, 1), :] = last
+            across = jnp.exp(rate[pl.ds(m, 1), lanes] * (-float(count)))
+            ends[slab, pl.ds(m, 1), :] = ends[slab, pl.ds(m, 1), :] + across * last
+
+
+def second_pass(band, slab, steps, modes, queries, product, starts, middle, before, rate, residue, bias, ordered):
     lanes = slab_lanes(slab)
     row = lax.broadcasted_iota(jnp.int32, (GROUPS, LANES), 0)
-    position = ((row + band * GROUPS) * steps).astype(jnp.float32)
+    position = (row * steps).astype(jnp.float32)
     decay, weight, state = [], [], []
     for m in range(modes):
         speed = wide(rate[pl.ds(m, 1), lanes])
         decay.append(jnp.exp(-speed))
         weight.append(wide(residue[pl.ds(m, 1), lanes]))
-        carried = jnp.exp(-speed * position) * wide(before[slab, pl.ds(m, 1), :])
+        entering = before[slab, pl.ds(m, 1), :]
+        if band:
+            across = jnp.exp(rate[pl.ds(m, 1), lanes] * (-float(steps * GROUPS)))
+            entering = across * entering + middle[slab, pl.ds(m, 1), :]
+        carried = jnp.exp(-speed * position) * wide(entering)
         state.append(starts[band, m, :, lanes] + carried)
     skip = wide(bias[pl.ds(0, 1), lanes])
     for i in range(steps):
@@ -122,6 +128,7 @@
     queries,
     product,
     starts,
+    middle,
     edge,
     halo,
     ends,
@@ -300,22 +307,50 @@
     weight_step(0)
     for copy in small:
         copy.wait()
+    keep = jnp.where(rank > 0, 1.0, 0.0)
+
+    def passed(band, slab):
+        first_pass(
+            band,
+            slab,
+            keep,
+            steps,
+            modes,
+            halo,
+            projected,
+            taps,
+            rate,
+            extended,
+            queries,
+            product,
+            starts,
+            middle,
+            ends,
+        )
+
+    @pl.loop(0, groups)
+    def _(n):
+        rows_in(n).wait()
+
+        @pl.when(n % 2 == 0)
+        def _():
+            weight_step(1 + n // 2)
+
+        @pl.loop(0, SCOPE)
+        def _(i):
+            passed(1, n * SCOPE + i)
+
     edge_copy.wait_recv()
-    keep = jnp.where(rank > 0, 1.0, 0.0)
 
     def all_but_one(ref, send_sem, recv_sem):
         view = ref.at[pl.ds(0, ranks - 1)]
         return remote(view, view, send_sem, recv_sem, lax.rem(rank + 1, ranks), z)
 
     def first_group(n):
-        rows_in(n).wait()
-
         @pl.loop(0, SCOPE)
         def _(i):
             slab = n * SCOPE + (i + rank) % SCOPE
-            first_pass(
-                slab, keep, steps, modes, halo, projected, taps, rate, extended, queries, product, starts, ends
-            )
+            passed(0, slab)
 
             @pl.when(slab == rank)
             def _():
@@ -358,7 +393,7 @@
         @pl.loop(0, SCOPE)
         def _(i):
             gathered[band, n, 0, :, slab_lanes(i)] = second_pass(
-                band, n * SCOPE + i, steps, modes, queries, product, starts, before, rate, residue, bias, ordered
+                band, n * SCOPE + i, steps, modes, queries, product, starts, middle, before, rate, residue, bias, ordered
             )
 
         rows_copy(band, n, 1, x_up).start()
@@ -367,11 +402,13 @@
 
     @pl.loop(0, groups)
     def _(n):
-        for i in range(PACE):
-            weight_step(n * PACE + 1 + i)
+        @pl.when(n % 2 == 0)
+        def _():
+            weight_step(1 + groups // 2 + n // 2)
+
         first_group((n + rank // SCOPE) % groups)
 
-    step = 1 + PACE * groups
+    step = 1 + groups
     weight_steps(step, step + AHEAD)
     scan()
     weight_steps(step + AHEAD, step + 2 * AHEAD)
@@ -506,6 +543,7 @@
             pltpu.VMEM((BANDS * steps, GROUPS, width), f32),
             pltpu.VMEM((BANDS * steps, GROUPS, width), f32),
             pltpu.VMEM((BANDS, modes, GROUPS, width), f32),
+            exchanged,
             pltpu.VMEM((8, width), f32),
             pltpu.VMEM((8, width), f32),
             exchanged,

time: 88.5 us -> 86.9 us (0.982)
  Pallas kernels: 85.3 us -> 84.2 us
    pallas_call x1, Pallas kernels: 85.3 us -> 84.2 us  [on_device(): pl.pallas_call(functools.partial(block_kernel, ranks, steps, modes), in_s...]
where the time goes in v6:
time: 86.9 us; the launch traced here: 86.5 us
  Pallas kernels  84.2 us (97%)
  local copies, waits for them, and re-layouts  2.26 us (3%)
    pallas_call x1, Pallas kernels, on_device(): pl.pallas_call(functools.partial(block_kernel, ranks, steps, modes), in_s...  84.2 us
    unnamed x1, local copies, waits for them, and re-layouts  2.26 us

profile of v6, /device:TPU:4, one launch (start us, length us, event | category | flops | bytes accessed | tf_op | source)
XLA Modules:
  0.0 86.5 jit_solution(396745299908310507)
XLA Ops:
  0.0 84.2 %shard_map.64 = bf16[8,128,512]{2,1,0:T(8,128)(2,1)} custom-call(bf16[3,128,4096]{2,1,0:T(8,128)(2,1)} %bitcast.2, f32[3,3,4096]{2,1,0:T(4,128)} %taps_in.1, f32[16,4096]{1,0:T(8,128)} %rate_in.1, f32[16,4096]{1,0:T(8,128)} %residue_in.1, f32[1,4096]{1,0:T(1,128)} %bitcast.3, bf16[4096,512]{1,0:T(8,128)(2,1)} %out_weight.1), custom_call_target="tpu_custom_call" | custom-call | tf_op jit(solution)/shard_map/pallas_call | solution.py:529
  84.3 2.3 %copy.8 = bf16[8,128,512]{2,1,0:T(8,128)(2,1)} copy(bf16[8,128,512]{2,1,0:T(8,128)(2,1)} %shard_map.64) | data formatting | bytes 2097152
